TPU v7x, 256 devices: a whole 4x4x8 slice. The times are simulated.
256 devices in a mesh: space: 8 (over y, core), vel: 32 (over z, x).
Axes of the slice: x: 4, y: 4, z: 8, core: 2. Of those that a mesh axis runs over, the one named last changes fastest.
Arguments:
- distribution: float32 [8, 256, 13824], P('space', None, 'vel'), may hold values from -6 to 6
- neighbours: int32 [8, 4], P('space'), may hold values from -1 to 7, as said below
- block_level: int32 [8], P('space'), may hold values from 0 to 2
- collide_mask: int32 [2048], P('space'), may hold values from 0 to 1, as said below
- gain_first: float32 [6, 13824], replicated, may hold values from -1.8 to 1.8
- gain_second: float32 [6, 13824], replicated, may hold values from -1.8 to 1.8
- loss_rates: float32 [13824], replicated, may hold values from 0.2 to 2
Outputs:
- distribution_next: float32 [8, 256, 13824], P('space', None, 'vel')
Inputs may be any that keep to these rules, and one draw needn't show every extreme that they name: `neighbours`: each entry is -1 or a block held by the same index of space as the block itself or by the index one below or one above (index s holds blocks s * 1 to (s + 1) - 1). `collide_mask`: the cells of one index of space (its 1 block) hold at most 128 ones, and some index holds exactly 128.
All inputs are finite; a program needn't handle non-finite values.
Results may differ from a plain program's by a relative error of at most 0.0003.
Values sent between devices are 32-bit elements; how exact they have to be, the bound alone decides.
No kernel may reach another device: no remote copies, remote signals or barrier semaphores. Data moves between devices by JAX's collectives and lax.ppermute only.
A program may use at most 128 MiB of HBM per device.

v0:
```python
import jax
import jax.numpy as jnp
import ml_dtypes
import numpy as np
from jax import lax
from jax.experimental import pallas as pl
from jax.experimental.pallas import tpu as pltpu
from jax.sharding import PartitionSpec as P

BSIDE = 16
VDIM = 24
CELLS = BSIDE * BSIDE
TERMS = 6
ACT = 128
LANES = 128
WIDTH = 432
TILES = 4
TAIL = WIDTH - 3 * LANES
GROUP = 32
OWN = ACT // GROUP
CHUNK = TILES * OWN
PLANE = VDIM * VDIM
EDGE = 5 * BSIDE
COURANT = 0.2
EPS = 1e-06

f32 = jnp.float32
bf16 = jnp.bfloat16


def hartley_pieces():
    k = np.arange(VDIM)
    angle = 2.0 * np.pi * ((k[:, None] * k[None, :]) % VDIM) / VDIM
    table = (np.cos(angle) + np.sin(angle)) / np.sqrt(VDIM)
    place = np.arange(VDIM)
    first = 3 * (place % 8) + place // 8

    def pieces(array):
        high = array.astype(ml_dtypes.bfloat16)
        low = (array - high.astype(np.float64)).astype(ml_dtypes.bfloat16)
        return jnp.asarray(high), jnp.asarray(low)

    plane = np.kron(table, table)
    forward = np.kron(np.eye(OWN), table[:, first])
    back = np.kron(np.eye(2 * OWN), table[first, :])
    return (*pieces(plane), *pieces(forward), *pieces(back))


def dot(a, b):
    return jnp.dot(a, b, preferred_element_type=f32)


def split(a):
    high = a.astype(bf16)
    return high, (a - high.astype(f32)).astype(bf16)


def product(a, b):
    return dot(a[0], b[0]) + dot(a[1], b[0]) + dot(a[0], b[1])


def velocity_lanes(tile):
    start = lax.axis_index("vel") * WIDTH + tile * LANES
    lane = lax.broadcasted_iota(jnp.int32, (8, LANES), 1)
    g = (start + lane).astype(f32)
    rows = jnp.floor((g + 0.5) * (1.0 / VDIM))
    first = jnp.floor((rows + 0.5) * (1.0 / VDIM))
    second = rows - VDIM * first
    half = (VDIM - 1) / 2.0
    return (first - half) / half, (second - half) / half


def upwind_steps(u):
    count = BSIDE
    d = [u[m + 1] - u[m] for m in range(count + 4)]
    low, mid, high, rise, fall, side = {}, {}, {}, {}, {}, {}
    twice = [a + a for a in d]
    for m in range(count + 3):
        left, right = d[m], d[m + 1]
        bend = right - left
        base = bend * bend * (13.0 / 3.0) + 4.0 * EPS
        rise[m] = twice[m + 1] + bend
        side[m] = left + right
        fall[m] = bend - twice[m]
        if m <= count:
            t = base + rise[m] * rise[m]
            low[m] = t * t
        if 1 <= m <= count + 1:
            t = base + side[m] * side[m]
            mid[m] = t * t
        if m >= 2:
            t = base + fall[m] * fall[m]
            high[m] = t * t
    values = []
    for i in range(count + 1):
        s0, s1, s2 = low[i], mid[i + 1], high[i + 2]
        d1, d2 = d[i + 1], d[i + 2]
        w0 = s1 * s2 * (1.0 / 3.0)
        w1 = s0 * s2 * 2.0
        w2 = s0 * s1
        p0 = rise[i] + rise[i] - d1
        p1 = side[i + 1] + d2
        p2 = d2 - fall[i + 2]
        top = w0 * p0 + w1 * p1 + w2 * p2
        values.append(u[i + 2] + top / (6.0 * (w0 + w1 + w2)))
    return [values[i + 1] - values[i] for i in range(count)]


def along(cells, lower, upper, neg, speed):
    wind = [jnp.where(neg, cells[BSIDE - 1 - i], cells[i]) for i in range(BSIDE)]
    u = [
        jnp.where(neg, upper[4], lower[4]),
        jnp.where(neg, upper[1], lower[2]),
        jnp.where(neg, upper[0], lower[3]),
        *wind,
        jnp.where(neg, lower[3], upper[0]),
        jnp.where(neg, lower[2], upper[1]),
    ]
    steps = [speed * s for s in upwind_steps(u)]
    return [jnp.where(neg, steps[BSIDE - 1 - i], steps[i]) for i in range(BSIDE)]


def row_cells(ref, tile, i, half):
    return ref[tile, i * BSIDE + 8 * half : i * BSIDE + 8 * half + 8, :]


def column_place(j, half):
    return pl.ds(8 * half * BSIDE + j, 8, stride=BSIDE)


def write_edges(cells_ref, edge_ref):
    for tile in range(TILES):
        first, second = velocity_lanes(tile)
        for half in range(2):
            for layer, i in enumerate((0, 1, 14, 15, None)):
                if i is None:
                    a = jnp.where(first < 0, row_cells(cells_ref, tile, 2, half), row_cells(cells_ref, tile, 13, half))
                    b = jnp.where(
                        second < 0,
                        cells_ref[tile, column_place(2, half), :],
                        cells_ref[tile, column_place(13, half), :],
                    )
                else:
                    a = row_cells(cells_ref, tile, i, half)
                    b = cells_ref[tile, column_place(i, half), :]
                at = layer * BSIDE + 8 * half
                if tile < TILES - 1:
                    base = tile * 2 * EDGE
                    edge_ref[base + at : base + at + 8, :] = a
                    edge_ref[base + EDGE + at : base + EDGE + at + 8, :] = b
                else:
                    base = tile * 2 * EDGE
                    lane = lax.broadcasted_iota(jnp.int32, (8, LANES), 1)
                    edge_ref[base + at : base + at + 8, :] = jnp.where(lane < 64, a, pltpu.roll(b, 64, 1))


def transport(neighbours, level, cells_ref, own_ref, a_ref, b_ref, change_ref, finish):
    me = lax.axis_index("space")
    partner = me + 1 - 2 * lax.rem(me, 2)
    ratio = COURANT * lax.shift_left(jnp.int32(1), level).astype(f32)

    def face_layers(face, base, half, shift):
        source = neighbours[0, face]
        from_own = source == me
        from_a = source == partner
        from_b = jnp.logical_and(source >= 0, jnp.logical_not(jnp.logical_or(from_own, from_a)))
        layers = []
        for layer in range(5):
            at = slice(base + layer * BSIDE + 8 * half, base + layer * BSIDE + 8 * half + 8)
            value = jnp.where(from_b, b_ref[at, :], 0.0)
            value = jnp.where(from_a, a_ref[at, :], value)
            value = jnp.where(from_own, own_ref[at, :], value)
            layers.append(pltpu.roll(value, 64, 1) if shift else value)
        return layers

    for tile in range(TILES):
        last = tile == TILES - 1
        first, second = velocity_lanes(tile)
        base = tile * 2 * EDGE
        for half in range(2):
            at = base if last else base + EDGE
            cells = [cells_ref[tile, column_place(j, half), :] for j in range(BSIDE)]
            lower = face_layers(2, at, half, last)
            upper = face_layers(3, at, half, last)
            change = along(cells, lower, upper, second < 0, jnp.abs(second))
            for j in range(BSIDE):
                change_ref[tile, column_place(j, half), :] = change[j]
        for half in range(2):
            cells = [row_cells(cells_ref, tile, i, half) for i in range(BSIDE)]
            lower = face_layers(0, base, half, False)
            upper = face_layers(1, base, half, False)
            change = along(cells, lower, upper, first < 0, jnp.abs(first))
            for i in range(BSIDE):
                total = row_cells(change_ref, tile, i, half) + change[i]
                finish(tile, i, half, cells[i], ratio * total)


def pack_kernel(x_ref, cells_ref, edge_ref):
    for tile in range(TILES - 1):
        cells_ref[tile] = x_ref[0, :, tile * LANES : (tile + 1) * LANES]
    cells_ref[TILES - 1] = jnp.zeros((CELLS, LANES), f32)
    cells_ref[TILES - 1, :, :TAIL] = x_ref[0, :, (TILES - 1) * LANES :]
    write_edges(cells_ref, edge_ref)


def first_kernel(near_ref, level_ref, x_ref, own_ref, a_ref, b_ref, out_ref, edge_ref, change_ref):
    def finish(tile, i, half, old, change):
        out_ref[tile, i * BSIDE + 8 * half : i * BSIDE + 8 * half + 8, :] = old - change

    transport(near_ref, level_ref[0], x_ref, own_ref, a_ref, b_ref, change_ref, finish)
    write_edges(out_ref, edge_ref)


def slots(mask_ref):
    marked = mask_ref[...].astype(f32)
    below = lax.broadcasted_iota(jnp.int32, (CELLS, CELLS), 0) <= lax.broadcasted_iota(jnp.int32, (CELLS, CELLS), 1)
    rank = dot(jnp.broadcast_to(marked, (8, CELLS)).astype(bf16), below.astype(f32).astype(bf16))[:1]
    slot = lax.broadcasted_iota(jnp.int32, (ACT, CELLS), 0).astype(f32) + 1.0
    hit = jnp.logical_and(slot == rank, marked > 0.5)
    return hit.astype(f32).astype(bf16)


def second_kernel(near_ref, level_ref, mask_ref, base_ref, x_ref, own_ref, a_ref, b_ref, out_ref, send_ref, change_ref):
    def finish(tile, i, half, old, change):
        start = row_cells(base_ref, tile, i, half)
        out_ref[tile, i * BSIDE + 8 * half : i * BSIDE + 8 * half + 8, :] = 0.5 * start + 0.5 * (old - change)

    transport(near_ref, level_ref[0], x_ref, own_ref, a_ref, b_ref, change_ref, finish)
    pick = slots(mask_ref)
    for pair in range(2):
        cells = jnp.concatenate([out_ref[2 * pair], out_ref[2 * pair + 1]], axis=1)
        high, low = split(cells)
        picked = dot(pick, high) + dot(pick, low)
        for side in range(2):
            for c in range(OWN):
                send_ref[pl.ds((2 * pair + side) * OWN + c, GROUP, stride=CHUNK), :] = picked[
                    c * GROUP : (c + 1) * GROUP, side * LANES : (side + 1) * LANES
                ]


def last_kernel(mask_ref, cells_ref, got_ref, out_ref):
    pick = slots(mask_ref)
    for pair in range(2):
        got = jnp.concatenate(
            [
                jnp.concatenate(
                    [got_ref[pl.ds(tile * OWN + c, GROUP, stride=CHUNK), :] for c in range(OWN)], axis=0
                )
                for tile in (2 * pair, 2 * pair + 1)
            ],
            axis=1,
        )
        high, low = split(got)
        put = lambda piece: lax.dot_general(pick, piece, (((0,), (0,)), ((), ())), preferred_element_type=f32)
        change = put(high) + put(low)
        for side in range(2):
            tile = 2 * pair + side
            wide = TAIL if tile == TILES - 1 else LANES
            out_ref[0, :, tile * LANES : tile * LANES + wide] = (
                cells_ref[tile] + change[:, side * LANES : (side + 1) * LANES]
            )[:, :wide]


def collide_kernel(
    got_ref, first_ref, second_ref, loss_ref, ph_ref, pl_ref, fh_ref, fl_ref, bh_ref, bl_ref, out_ref, x_ref, gain_ref
):
    rows = OWN * VDIM
    for c in range(OWN):
        part = []
        for m in range(4):
            tiles = [got_ref[pl.ds(m * CHUNK + t * OWN + c, 8, stride=4 * CHUNK), :] for t in range(TILES)]
            part.append(jnp.concatenate([*tiles[:3], tiles[3][:, :TAIL]], axis=1))
        x_ref[c * VDIM : c * VDIM + 8, :] = jnp.concatenate([part[0], part[1][:, :144]], axis=1)
        x_ref[c * VDIM + 8 : c * VDIM + 16, :] = jnp.concatenate([part[1][:, 144:], part[2][:, :288]], axis=1)
        x_ref[c * VDIM + 16 : c * VDIM + 24, :] = jnp.concatenate([part[2][:, 288:], part[3]], axis=1)
    plane = (ph_ref[...], pl_ref[...])
    spectrum = product(split(x_ref[...]), plane)
    spectrum = product((fh_ref[...], fl_ref[...]), split(spectrum))

    def weighted(table):
        return jnp.concatenate([spectrum[c * VDIM : (c + 1) * VDIM] * table for c in range(OWN)], axis=0)

    back = (bh_ref[...], bl_ref[...])
    gain_ref[...] = jnp.zeros_like(gain_ref)
    for t in range(TERMS):
        scaled = jnp.concatenate([weighted(first_ref[t]), weighted(second_ref[t])], axis=0)
        image = product(back, split(product(split(scaled), plane)))
        gain_ref[...] += image[:rows] * image[rows:]
    image = product(
        (bh_ref[:rows, :rows], bl_ref[:rows, :rows]), split(product(split(weighted(loss_ref[...])), plane))
    )
    gain_ref[...] = gain_ref[...] - x_ref[...] * image
    for c in range(OWN):
        r0 = gain_ref[c * VDIM : c * VDIM + 8, :]
        r1 = gain_ref[c * VDIM + 8 : c * VDIM + 16, :]
        r2 = gain_ref[c * VDIM + 16 : c * VDIM + 24, :]
        part = [
            r0[:, :WIDTH],
            jnp.concatenate([r0[:, WIDTH:], r1[:, :288]], axis=1),
            jnp.concatenate([r1[:, 288:], r2[:, :144]], axis=1),
            r2[:, 144:],
        ]
        blank = jnp.zeros((8, LANES - TAIL), f32)
        for m in range(4):
            for t in range(TILES):
                piece = part[m][:, t * LANES : min((t + 1) * LANES, WIDTH)]
                if t == TILES - 1:
                    piece = jnp.concatenate([piece, blank], axis=1)
                out_ref[pl.ds(m * CHUNK + t * OWN + c, 8, stride=4 * CHUNK), :] = piece


SMALL = pl.BlockSpec(memory_space=pltpu.SMEM)
BIG = pl.BlockSpec(memory_space=pltpu.VMEM)
PARAMS = pltpu.CompilerParams(vmem_limit_bytes=48 * 1024 * 1024)


def shape(*dims):
    return jax.ShapeDtypeStruct(dims, f32)


def call(kernel, small, big, outs, scratch=(), name=None):
    return pl.pallas_call(
        kernel,
        out_shape=outs,
        in_specs=[SMALL] * len(small) + [BIG] * len(big),
        out_specs=jax.tree.map(lambda _: BIG, outs),
        scratch_shapes=list(scratch),
        compiler_params=PARAMS,
        name=name,
    )(*small, *big)


def swap_edges(edge):
    count = lax.axis_size("space")
    pair = [(i, i ^ 1) for i in range(count)]
    other = [(i, (((i + 1) ^ 1) - 1) % count) for i in range(count)]
    return lax.ppermute(edge, "space", pair), lax.ppermute(edge, "space", other)


def shards(
    distribution, neighbours, block_level, collide_mask, gain_first, gain_second, loss_rates
):
    pieces = hartley_pieces()
    tiles = shape(TILES, CELLS, LANES)
    edges = shape(7 * EDGE, LANES)
    packed = shape(GROUP * CHUNK, LANES)
    change = pltpu.VMEM((TILES, CELLS, LANES), f32)
    mask = collide_mask.reshape(1, CELLS)

    cells, edge = call(pack_kernel, [], [distribution], (tiles, edges), name="pack_edges")
    near_a, near_b = swap_edges(edge)
    one, edge_one = call(
        first_kernel,
        [neighbours, block_level],
        [cells, edge, near_a, near_b],
        (tiles, edges),
        [change],
        name="first_section",
    )
    near_a, near_b = swap_edges(edge_one)
    two, send = call(
        second_kernel,
        [neighbours, block_level],
        [mask, cells, one, edge_one, near_a, near_b],
        (tiles, packed),
        [change],
        name="second_section",
    )
    got = lax.all_to_all(send, "vel", split_axis=0, concat_axis=0, tiled=True)
    collided = call(
        collide_kernel,
        [],
        [
            got,
            gain_first.reshape(TERMS, VDIM, PLANE),
            gain_second.reshape(TERMS, VDIM, PLANE),
            loss_rates.reshape(VDIM, PLANE),
            *pieces,
        ],
        packed,
        [pltpu.VMEM((OWN * VDIM, PLANE), f32)] * 2,
        name="collide",
    )
    back = lax.all_to_all(collided, "vel", split_axis=0, concat_axis=0, tiled=True)
    return call(
        last_kernel, [], [mask, two, back], shape(1, CELLS, WIDTH), name="add_collision"
    )


def solution(mesh):
    in_specs = (P("space", None, "vel"), P("space", None), P("space"), P("space"), P(), P(), P())
    out_specs = P("space", None, "vel")
    return jax.shard_map(shards, mesh=mesh, in_specs=in_specs, out_specs=out_specs, check_vma=False)
```

profile of v0, /device:TPU:24, one launch (start us, length us, event | category | flops | bytes accessed | tf_op | source)
XLA Modules:
  0.0 74.0 jit_solution(9116203455806575928)
XLA Ops:
  0.0 1.2 %copy.14.x_ref = f32[1,256,432]{2,1,0:T(8,128)S(1)} copy(f32[1,256,432]{1,2,0:T(8,128)} %param.13) | data formatting | bytes 884736 | tf_op args[0]
  1.2 0.2 pack_edges.1
  1.4 0.0 collective-permute-start
  1.4 0.8 %collective-permute-start.1 = (f32[560,128]{1,0:T(8,128)S(1)}, f32[560,128]{1,0:T(8,128)S(1)}, u32[]{:S(2)}, u32[]{:S(2)}) collective-permute-start(f32[560,128]{1,0:T(8,128)S(1)} %get-tuple-element.12.own_ref), channel_id=1, source_target_pairs={{0,224},{32,64},{64,32},{96,128},{128,96},{160,192},{192,160},{224... | collective-permute-start | bytes 860168 | tf_op jit(solution)/shard_map/ppermute | solution.py:337
  2.9 0.0 copy-start.7
  2.9 0.0 collective-permute-done.a_ref
  3.0 4.6 %collective-permute-done.1.b_ref = f32[560,128]{1,0:T(8,128)S(1)} collective-permute-done((f32[560,128]{1,0:T(8,128)S(1)}, f32[560,128]{1,0:T(8,128)S(1)}, u32[]{:S(2)}, u32[]{:S(2)}) %collective-permute-start.1) | collective-permute-done | bytes 286752 | tf_op jit(solution)/shard_map/ppermute | solution.py:337
  7.6 0.0 copy-done.7
  7.6 2.6 %first_section.1 = (f32[4,256,128]{2,1,0:T(8,128)S(1)}, f32[560,128]{1,0:T(8,128)S(1)}) custom-call(s32[1,4]{1,0:T(1,128)S(1)} %copy-done.7, s32[1]{0:T(128)S(6)} %copy.16.level_ref, f32[4,256,128]{2,1,0:T(8,128)S(1)} %get-tuple-element.11.x_ref.base_ref, f32[560,128]{1,0:T(8,128)S(1)} %get-tuple-element.12.own_ref, ...), custom_call_target="tpu_custom_call" | custom-call | tf_op jit(solution)/shard_map/first_section/pallas_call | solution.py:322
  10.1 1.7 %collective-permute-start.2 = (f32[560,128]{1,0:T(8,128)S(1)}, f32[560,128]{1,0:T(8,128)S(1)}, u32[]{:S(2)}, u32[]{:S(2)}) collective-permute-start(f32[560,128]{1,0:T(8,128)S(1)} %get-tuple-element.14.own_ref), channel_id=1, source_target_pairs={{0,32},{32,0},{64,96},{96,64},{128,160},{160,128},{192,224},{224,1... | collective-permute-start | bytes 860168 | tf_op jit(solution)/shard_map/ppermute | solution.py:337
  11.8 0.0 collective-permute-start.3
  11.8 1.2 %collective-permute-done.2.a_ref = f32[560,128]{1,0:T(8,128)S(1)} collective-permute-done((f32[560,128]{1,0:T(8,128)S(1)}, f32[560,128]{1,0:T(8,128)S(1)}, u32[]{:S(2)}, u32[]{:S(2)}) %collective-permute-start.2) | collective-permute-done | bytes 286752 | tf_op jit(solution)/shard_map/ppermute | solution.py:337
  13.0 4.9 %collective-permute-done.3.b_ref = f32[560,128]{1,0:T(8,128)S(1)} collective-permute-done((f32[560,128]{1,0:T(8,128)S(1)}, f32[560,128]{1,0:T(8,128)S(1)}, u32[]{:S(2)}, u32[]{:S(2)}) %collective-permute-start.3) | collective-permute-done | bytes 286752 | tf_op jit(solution)/shard_map/ppermute | solution.py:337
  17.9 0.0 copy-start.6
  17.9 0.7 copy-done.6
  18.6 3.5 %second_section.1 = (f32[4,256,128]{2,1,0:T(8,128)S(1)}, f32[512,128]{1,0:T(8,128)}) custom-call(s32[1,4]{1,0:T(1,128)S(1)} %copy-done.7, s32[1]{0:T(128)S(6)} %copy.16.level_ref, s32[1,256]{1,0:T(1,128)S(1)} %bitcast.8, f32[4,256,128]{2,1,0:T(8,128)S(1)} %get-tuple-element.11.x_ref.base_ref, f32[4,256,128]{2,1,0:T(8,128)S(1)} %get-tuple-element.13.x_ref, ...), custom_call_target="tpu_custom_call" | custom-call | tf_op jit(solution)/shard_map/second_section/pallas_call | solution.py:322
  22.1 0.0 copy-start.8
  22.1 0.0 copy-start.9
  22.1 11.6 %all-to-all-start = ((f32[32,16,128]{2,1,0:T(8,128)}), f32[32,16,128]{2,1,0:T(8,128)S(1)}, u32[]{:S(2)}, u32[]{:S(2)}) async-start(f32[32,16,128]{2,1,0:T(8,128)} %bitcast.1), calls=%async_computation | async-start | bytes 524288 | tf_op jit(solution)/shard_map/all_to_all | solution.py:369
  33.7 0.0 copy-done.8
  33.7 0.0 copy-start
  33.7 0.0 copy-start.1
  33.8 0.1 reshape.17.first_ref
  33.9 0.0 copy-start.3
  33.9 0.0 copy-start.4
  33.9 0.0 copy-start.5
  33.9 1.2 %reshape.18.second_ref = f32[6,24,576]{2,1,0:T(8,128)S(1)} reshape(f32[6,13824]{1,0:T(8,128)} %param.18) | data formatting | bytes 663552 | tf_op jit(solution)/shard_map/reshape | solution.py:376
  35.2 0.0 copy-done.9
  35.2 0.0 copy-start.2
  35.2 0.1 reshape.19.loss_ref
  35.3 12.1 %all-to-all-done = f32[32,16,128]{2,1,0:T(8,128)S(1)} async-done(((f32[32,16,128]{2,1,0:T(8,128)}), f32[32,16,128]{2,1,0:T(8,128)S(1)}, u32[]{:S(2)}, u32[]{:S(2)}) %all-to-all-start) | async-done | bytes 262176 | tf_op jit(solution)/shard_map/all_to_all | solution.py:369
  47.4 0.0 copy-done
  47.4 0.0 copy-done.1
  47.4 0.0 copy-done.3
  47.4 0.0 copy-done.4
  47.4 0.0 copy-done.5
  47.4 0.0 copy-done.2
  47.4 8.0 %collide.1 = f32[512,128]{1,0:T(8,128)S(1)} custom-call(f32[512,128]{1,0:T(8,128)S(1)} %bitcast.5, f32[6,24,576]{2,1,0:T(8,128)S(1)} %reshape.17.first_ref, f32[6,24,576]{2,1,0:T(8,128)S(1)} %reshape.18.second_ref, f32[24,576]{1,0:T(8,128)S(1)} %reshape.19.loss_ref, bf16[576,576]{1,0:T(8,128)(2,1)S(1)} %copy-done, bf16[576,576]{1,0:T(8,128)(2,1)S(1)} %copy-done.1, ...), custom_call_target="tpu_custom_call" | custom-call | tf_op jit(solution)/shard_map/collide/pallas_call | solution.py:322
  55.4 17.1 %all_to_all.22 = f32[32,16,128]{2,1,0:T(8,128)S(1)} all-to-all(f32[32,16,128]{2,1,0:T(8,128)S(1)} %bitcast.6), channel_id=1, replica_groups=mesh['space'=8,'vel'=32] {'vel'}, dimensions={0} | all-to-all | bytes 524288 | tf_op jit(solution)/shard_map/all_to_all | solution.py:384
  72.6 0.5 add_collision.1
  73.1 0.9 %copy.15 = f32[1,256,432]{1,2,0:T(8,128)} copy(f32[1,256,432]{2,1,0:T(8,128)S(1)} %add_collision.1) | data formatting | bytes 884736 | tf_op jit(solution)/shard_map/add_collision/pallas_call | solution.py:322
Async XLA Ops:
  1.4 1.6 %collective-permute-start = (f32[560,128]{1,0:T(8,128)S(1)}, f32[560,128]{1,0:T(8,128)S(1)}, u32[]{:S(2)}, u32[]{:S(2)}) collective-permute-start(f32[560,128]{1,0:T(8,128)S(1)} %get-tuple-element.12.own_ref), channel_id=1, source_target_pairs={{0,32},{32,0},{64,96},{96,64},{128,160},{160,128},{192,224},{224,1... | collective-permute-start | bytes 860168 | tf_op jit(solution)/shard_map/ppermute | solution.py:337
  1.4 6.1 %collective-permute-start.1 = (f32[560,128]{1,0:T(8,128)S(1)}, f32[560,128]{1,0:T(8,128)S(1)}, u32[]{:S(2)}, u32[]{:S(2)}) collective-permute-start(f32[560,128]{1,0:T(8,128)S(1)} %get-tuple-element.12.own_ref), channel_id=1, source_target_pairs={{0,224},{32,64},{64,32},{96,128},{128,96},{160,192},{192,160},{224... | collective-permute-start | bytes 860168 | tf_op jit(solution)/shard_map/ppermute | solution.py:337
  2.9 4.7 %copy-start.7 = (s32[1,4]{1,0:T(1,128)S(1)}, s32[1,4]{1,0:T(1,128)}, u32[]{:S(2)}) copy-start(s32[1,4]{1,0:T(1,128)} %near_ref.3) | copy-start | bytes 52
  10.1 2.9 %collective-permute-start.2 = (f32[560,128]{1,0:T(8,128)S(1)}, f32[560,128]{1,0:T(8,128)S(1)}, u32[]{:S(2)}, u32[]{:S(2)}) collective-permute-start(f32[560,128]{1,0:T(8,128)S(1)} %get-tuple-element.14.own_ref), channel_id=1, source_target_pairs={{0,32},{32,0},{64,96},{96,64},{128,160},{160,128},{192,224},{224,1... | collective-permute-start | bytes 860168 | tf_op jit(solution)/shard_map/ppermute | solution.py:337
  11.8 6.1 %collective-permute-start.3 = (f32[560,128]{1,0:T(8,128)S(1)}, f32[560,128]{1,0:T(8,128)S(1)}, u32[]{:S(2)}, u32[]{:S(2)}) collective-permute-start(f32[560,128]{1,0:T(8,128)S(1)} %get-tuple-element.14.own_ref), channel_id=1, source_target_pairs={{0,224},{32,64},{64,32},{96,128},{128,96},{160,192},{192,160},{224... | collective-permute-start | bytes 860168 | tf_op jit(solution)/shard_map/ppermute | solution.py:337
  17.9 0.7 copy-start.6
  22.1 11.6 %copy-start.8 = (f32[6,13824]{1,0:T(8,128)S(1)}, f32[6,13824]{1,0:T(8,128)}, u32[]{:S(2)}) copy-start(f32[6,13824]{1,0:T(8,128)} %param.17) | copy-start | bytes 995332
  22.1 13.1 %copy-start.9 = (f32[13824]{0:T(1024)S(1)}, f32[13824]{0:T(1024)}, u32[]{:S(2)}) copy-start(f32[13824]{0:T(1024)} %param.19) | copy-start | bytes 165892
  22.1 25.3 %all-to-all-start = ((f32[32,16,128]{2,1,0:T(8,128)}), f32[32,16,128]{2,1,0:T(8,128)S(1)}, u32[]{:S(2)}, u32[]{:S(2)}) async-start(f32[32,16,128]{2,1,0:T(8,128)} %bitcast.1), calls=%async_computation | async-start | bytes 524288 | tf_op jit(solution)/shard_map/all_to_all | solution.py:369
  33.7 13.6 %copy-start = (bf16[576,576]{1,0:T(8,128)(2,1)S(1)}, bf16[576,576]{1,0:T(8,128)(2,1)}, u32[]{:S(2)}) copy-start(bf16[576,576]{1,0:T(8,128)(2,1)} %constant.12.clone.ph_ref) | copy-start | bytes 1990660
  33.7 13.6 %copy-start.1 = (bf16[576,576]{1,0:T(8,128)(2,1)S(1)}, bf16[576,576]{1,0:T(8,128)(2,1)}, u32[]{:S(2)}) copy-start(bf16[576,576]{1,0:T(8,128)(2,1)} %constant.13.clone.pl_ref) | copy-start | bytes 1990660
  33.9 13.5 %copy-start.3 = (bf16[192,192]{1,0:T(8,128)(2,1)S(1)}, bf16[192,192]{1,0:T(8,128)(2,1)}, u32[]{:S(2)}) copy-start(bf16[192,192]{1,0:T(8,128)(2,1)} %constant.17.clone.bl_ref) | copy-start | bytes 221188
  33.9 13.5 %copy-start.4 = (bf16[96,96]{1,0:T(8,128)(2,1)S(1)}, bf16[96,96]{1,0:T(8,128)(2,1)}, u32[]{:S(2)}) copy-start(bf16[96,96]{1,0:T(8,128)(2,1)} %constant.14.clone.fh_ref) | copy-start | bytes 55300
  33.9 13.5 %copy-start.5 = (bf16[96,96]{1,0:T(8,128)(2,1)S(1)}, bf16[96,96]{1,0:T(8,128)(2,1)}, u32[]{:S(2)}) copy-start(bf16[96,96]{1,0:T(8,128)(2,1)} %constant.15.clone.fl_ref) | copy-start | bytes 55300
  35.2 12.2 %copy-start.2 = (bf16[192,192]{1,0:T(8,128)(2,1)S(1)}, bf16[192,192]{1,0:T(8,128)(2,1)}, u32[]{:S(2)}) copy-start(bf16[192,192]{1,0:T(8,128)(2,1)} %constant.16.clone.bh_ref) | copy-start | bytes 221188
where the time goes:
time: 74.3 us; the launch traced here: 74 us
  waiting for transfers between devices  22.8 us (31%)
  blocking collectives  17.1 us (23%)
  Pallas kernels  14.7 us (20%)
  starting transfers between devices  14.2 us (19%)
  local copies, waits for them, and re-layouts  4.33 us (6%)
  between operations  0.82 us (1%)
    all_to_all x1, blocking collectives, shards(): lax.all_to_all(collided, 'vel', split_axis=0, concat_axis=0, tiled=True)  17.1 us
    pallas_call x5, Pallas kernels, call(): pl.pallas_call(kernel, out_shape=outs, in_specs=[SMALL] * len(small) + [B...  14.7 us
    all_to_all x1, waiting for transfers between devices, shards(): got = lax.all_to_all(send, 'vel', split_axis=0, concat_axis=0, tiled=True)  12.1 us
    all_to_all x1, starting transfers between devices, shards(): got = lax.all_to_all(send, 'vel', split_axis=0, concat_axis=0, tiled=True)  11.6 us
    ppermute x2, waiting for transfers between devices, swap_edges(): lax.ppermute(edge, 'space', other)  9.45 us
    unnamed x21, local copies, waits for them, and re-layouts  1.94 us
    ppermute x2, starting transfers between devices, swap_edges(): lax.ppermute(edge, 'space', pair)  1.73 us
  transfers between devices with their start and end apart: 5, of which 4 were waited for; matrix products, arithmetic and copies ran while one was open for 2% of the time, Pallas kernels for 0%

commit v1 on v0

--- a/solution.py
+++ b/solution.py
@@ -28,6 +28,15 @@
 bf16 = jnp.bfloat16
 
 
+HALF = VDIM // 2
+QUARTER = HALF * HALF
+WIDE = 5 * LANES
+
+
+def quarter_lane(quarter, place):
+    return np.where(place < LANES, quarter * LANES + place, 4 * LANES + quarter * 16 + place - LANES)
+
+
 def hartley_pieces():
     k = np.arange(VDIM)
     angle = 2.0 * np.pi * ((k[:, None] * k[None, :]) % VDIM) / VDIM
@@ -40,10 +49,36 @@
         low = (array - high.astype(np.float64)).astype(ml_dtypes.bfloat16)
         return jnp.asarray(high), jnp.asarray(low)
 
-    plane = np.kron(table, table)
+    j, c = np.divmod(np.arange(PLANE), VDIM)
+    physical = np.zeros((PLANE, WIDE))
+    physical[
+        np.arange(PLANE), quarter_lane(2 * (j // HALF) + c // HALF, (j % HALF) * HALF + c % HALF)
+    ] = 1.0
+    spectral = np.zeros((PLANE, WIDE))
+    spectral[np.arange(PLANE), quarter_lane(2 * (j % 2) + c % 2, (j // 2) * HALF + c // 2)] = 1.0
+
+    blocks = np.zeros((4, 2 * LANES, 2 * LANES))
+    spot = np.arange(QUARTER)
+    for q in range(4):
+        jp, kp = divmod(q, 2)
+        block = np.kron(table[:HALF, jp::2], table[:HALF, kp::2])
+        column = np.where(spot < LANES, spot, LANES + 16 * q + spot - LANES)
+        blocks[q][np.ix_(np.arange(LANES), column)] = block[:LANES]
+        for g in range(4):
+            jh, kh = divmod(g, 2)
+            row = LANES + 16 * g + np.arange(QUARTER - LANES)
+            blocks[q][np.ix_(row, column)] = (-1.0) ** (jh * jp + kh * kp) * block[LANES:]
     forward = np.kron(np.eye(OWN), table[:, first])
     back = np.kron(np.eye(2 * OWN), table[first, :])
-    return (*pieces(plane), *pieces(forward), *pieces(back))
+    return dict(
+        place=jnp.asarray(physical.astype(ml_dtypes.bfloat16)),
+        unplace=jnp.asarray(physical.T.astype(ml_dtypes.bfloat16)),
+        order=jnp.asarray(spectral.astype(ml_dtypes.bfloat16)),
+        plane_forward=pieces(blocks),
+        plane_back=pieces(blocks.transpose(0, 2, 1)),
+        row_forward=pieces(forward),
+        row_back=pieces(back),
+    )
 
 
 def dot(a, b):
@@ -70,29 +105,29 @@
     return (first - half) / half, (second - half) / half
 
 
-def upwind_steps(u):
-    count = BSIDE
-    d = [u[m + 1] - u[m] for m in range(count + 4)]
+def interface_values(u):
+    count = len(u) - 4
+    d = [u[m + 1] - u[m] for m in range(count + 3)]
+    twice = [a + a for a in d]
     low, mid, high, rise, fall, side = {}, {}, {}, {}, {}, {}
-    twice = [a + a for a in d]
-    for m in range(count + 3):
+    for m in range(count + 2):
         left, right = d[m], d[m + 1]
         bend = right - left
         base = bend * bend * (13.0 / 3.0) + 4.0 * EPS
-        rise[m] = twice[m + 1] + bend
-        side[m] = left + right
-        fall[m] = bend - twice[m]
-        if m <= count:
+        if m < count:
+            rise[m] = twice[m + 1] + bend
             t = base + rise[m] * rise[m]
             low[m] = t * t
-        if 1 <= m <= count + 1:
+        if 1 <= m <= count:
+            side[m] = left + right
             t = base + side[m] * side[m]
             mid[m] = t * t
         if m >= 2:
+            fall[m] = bend - twice[m]
             t = base + fall[m] * fall[m]
             high[m] = t * t
     values = []
-    for i in range(count + 1):
+    for i in range(count):
         s0, s1, s2 = low[i], mid[i + 1], high[i + 2]
         d1, d2 = d[i + 1], d[i + 2]
         w0 = s1 * s2 * (1.0 / 3.0)
@@ -103,21 +138,47 @@
         p2 = d2 - fall[i + 2]
         top = w0 * p0 + w1 * p1 + w2 * p2
         values.append(u[i + 2] + top / (6.0 * (w0 + w1 + w2)))
-    return [values[i + 1] - values[i] for i in range(count)]
-
-
-def along(cells, lower, upper, neg, speed):
+    return values
+
+
+def inner_steps(cells, neg):
     wind = [jnp.where(neg, cells[BSIDE - 1 - i], cells[i]) for i in range(BSIDE)]
-    u = [
-        jnp.where(neg, upper[4], lower[4]),
-        jnp.where(neg, upper[1], lower[2]),
-        jnp.where(neg, upper[0], lower[3]),
-        *wind,
-        jnp.where(neg, lower[3], upper[0]),
-        jnp.where(neg, lower[2], upper[1]),
+    values = interface_values(wind)
+    return {
+        0: values[0],
+        BSIDE - 1: values[-1],
+        **{i: values[i - 2] - values[i - 3] for i in range(3, BSIDE - 2)},
+    }
+
+
+def finished_steps(inner, cells, lower, upper, neg, speed):
+    n = BSIDE
+    wind = {i: jnp.where(neg, cells[n - 1 - i], cells[i]) for i in (0, 1, 2, 3, n - 4, n - 3, n - 2, n - 1)}
+    start = interface_values(
+        [
+            jnp.where(neg, upper[4], lower[4]),
+            jnp.where(neg, upper[1], lower[2]),
+            jnp.where(neg, upper[0], lower[3]),
+            *[wind[i] for i in range(4)],
+        ]
+    )
+    end = interface_values(
+        [
+            *[wind[i] for i in range(n - 4, n)],
+            jnp.where(neg, lower[3], upper[0]),
+            jnp.where(neg, lower[2], upper[1]),
+        ]
+    )
+    steps = [
+        start[1] - start[0],
+        start[2] - start[1],
+        inner[0] - start[2],
+        *[inner[i] for i in range(3, n - 2)],
+        end[0] - inner[n - 1],
+        end[1] - end[0],
     ]
-    steps = [speed * s for s in upwind_steps(u)]
-    return [jnp.where(neg, steps[BSIDE - 1 - i], steps[i]) for i in range(BSIDE)]
+    steps = [speed * s for s in steps]
+    return [jnp.where(neg, steps[n - 1 - i], steps[i]) for i in range(n)]
 
 
 def row_cells(ref, tile, i, half):
@@ -154,7 +215,23 @@
                     edge_ref[base + at : base + at + 8, :] = jnp.where(lane < 64, a, pltpu.roll(b, 64, 1))
 
 
-def transport(neighbours, level, cells_ref, own_ref, a_ref, b_ref, change_ref, finish):
+def inner_kernel(cells_ref, inner_ref):
+    for tile in range(TILES):
+        first, second = velocity_lanes(tile)
+        for half in range(2):
+            rows = slice(8 * half, 8 * half + 8)
+            cells = [cells_ref[tile, column_place(j, half), :] for j in range(BSIDE)]
+            for slot, value in inner_steps(cells, second < 0).items():
+                inner_ref[1, tile, slot, rows, :] = value
+            cells = [row_cells(cells_ref, tile, i, half) for i in range(BSIDE)]
+            for slot, value in inner_steps(cells, first < 0).items():
+                inner_ref[0, tile, slot, rows, :] = value
+
+
+SLOTS = (0, *range(3, BSIDE - 2), BSIDE - 1)
+
+
+def transport(neighbours, level, cells_ref, inner_ref, own_ref, a_ref, b_ref, change_ref, finish):
     me = lax.axis_index("space")
     partner = me + 1 - 2 * lax.rem(me, 2)
     ratio = COURANT * lax.shift_left(jnp.int32(1), level).astype(f32)
@@ -182,32 +259,35 @@
             cells = [cells_ref[tile, column_place(j, half), :] for j in range(BSIDE)]
             lower = face_layers(2, at, half, last)
             upper = face_layers(3, at, half, last)
-            change = along(cells, lower, upper, second < 0, jnp.abs(second))
+            inner = {slot: inner_ref[1, tile, slot, 8 * half : 8 * half + 8, :] for slot in SLOTS}
+            change = finished_steps(inner, cells, lower, upper, second < 0, jnp.abs(second))
             for j in range(BSIDE):
                 change_ref[tile, column_place(j, half), :] = change[j]
         for half in range(2):
             cells = [row_cells(cells_ref, tile, i, half) for i in range(BSIDE)]
             lower = face_layers(0, base, half, False)
             upper = face_layers(1, base, half, False)
-            change = along(cells, lower, upper, first < 0, jnp.abs(first))
+            inner = {slot: inner_ref[0, tile, slot, 8 * half : 8 * half + 8, :] for slot in SLOTS}
+            change = finished_steps(inner, cells, lower, upper, first < 0, jnp.abs(first))
             for i in range(BSIDE):
                 total = row_cells(change_ref, tile, i, half) + change[i]
                 finish(tile, i, half, cells[i], ratio * total)
 
 
 def pack_kernel(x_ref, cells_ref, edge_ref):
-    for tile in range(TILES - 1):
-        cells_ref[tile] = x_ref[0, :, tile * LANES : (tile + 1) * LANES]
-    cells_ref[TILES - 1] = jnp.zeros((CELLS, LANES), f32)
-    cells_ref[TILES - 1, :, :TAIL] = x_ref[0, :, (TILES - 1) * LANES :]
+    for tile in range(TILES):
+        piece = x_ref[0, tile * LANES : min((tile + 1) * LANES, WIDTH), :]
+        if tile == TILES - 1:
+            piece = jnp.concatenate([piece, jnp.zeros((LANES - TAIL, CELLS), f32)], axis=0)
+        cells_ref[tile] = piece.T
     write_edges(cells_ref, edge_ref)
 
 
-def first_kernel(near_ref, level_ref, x_ref, own_ref, a_ref, b_ref, out_ref, edge_ref, change_ref):
+def first_kernel(near_ref, level_ref, x_ref, inner_ref, own_ref, a_ref, b_ref, out_ref, edge_ref, change_ref):
     def finish(tile, i, half, old, change):
         out_ref[tile, i * BSIDE + 8 * half : i * BSIDE + 8 * half + 8, :] = old - change
 
-    transport(near_ref, level_ref[0], x_ref, own_ref, a_ref, b_ref, change_ref, finish)
+    transport(near_ref, level_ref[0], x_ref, inner_ref, own_ref, a_ref, b_ref, change_ref, finish)
     write_edges(out_ref, edge_ref)
 
 
@@ -220,13 +300,20 @@
     return hit.astype(f32).astype(bf16)
 
 
-def second_kernel(near_ref, level_ref, mask_ref, base_ref, x_ref, own_ref, a_ref, b_ref, out_ref, send_ref, change_ref):
+def inner_slots_kernel(mask_ref, cells_ref, inner_ref, pick_ref):
+    inner_kernel(cells_ref, inner_ref)
+    pick_ref[...] = slots(mask_ref)
+
+
+def second_kernel(
+    near_ref, level_ref, pick_ref, base_ref, x_ref, inner_ref, own_ref, a_ref, b_ref, out_ref, send_ref, change_ref
+):
     def finish(tile, i, half, old, change):
         start = row_cells(base_ref, tile, i, half)
         out_ref[tile, i * BSIDE + 8 * half : i * BSIDE + 8 * half + 8, :] = 0.5 * start + 0.5 * (old - change)
 
-    transport(near_ref, level_ref[0], x_ref, own_ref, a_ref, b_ref, change_ref, finish)
-    pick = slots(mask_ref)
+    transport(near_ref, level_ref[0], x_ref, inner_ref, own_ref, a_ref, b_ref, change_ref, finish)
+    pick = pick_ref[...]
     for pair in range(2):
         cells = jnp.concatenate([out_ref[2 * pair], out_ref[2 * pair + 1]], axis=1)
         high, low = split(cells)
@@ -238,8 +325,8 @@
                 ]
 
 
-def last_kernel(mask_ref, cells_ref, got_ref, out_ref):
-    pick = slots(mask_ref)
+def last_kernel(pick_ref, cells_ref, got_ref, out_ref):
+    pick = pick_ref[...]
     for pair in range(2):
         got = jnp.concatenate(
             [
@@ -256,13 +343,61 @@
         for side in range(2):
             tile = 2 * pair + side
             wide = TAIL if tile == TILES - 1 else LANES
-            out_ref[0, :, tile * LANES : tile * LANES + wide] = (
-                cells_ref[tile] + change[:, side * LANES : (side + 1) * LANES]
-            )[:, :wide]
+            total = cells_ref[tile] + change[:, side * LANES : (side + 1) * LANES]
+            out_ref[0, tile * LANES : tile * LANES + wide, :] = total.T[:wide]
+
+
+def order_kernel(first_ref, second_ref, loss_ref, order_ref, first_out, second_out, loss_out):
+    order = order_ref[...]
+    for table, out in ((first_ref, first_out), (second_ref, second_out), (loss_ref, loss_out)):
+        high, low = split(table[...])
+        out[...] = dot(high, order) + dot(low, order)
+
+
+def quarters(wide):
+    return [wide[:, q * LANES : (q + 1) * LANES] for q in range(5)]
+
+
+def mixed(mains):
+    a, b, c, d = mains
+    e, f, g, h = a + b, a - b, c + d, c - d
+    return [e + g, f + h, e - g, f - h]
+
+
+def plane_product(tiles, high_ref, low_ref):
+    parts = [split(t) for t in tiles]
+    mains, shared = [], None
+    for q in range(4):
+        high = jnp.concatenate([parts[q][0], parts[4][0]], axis=1)
+        low = jnp.concatenate([parts[q][1], parts[4][1]], axis=1)
+        both = product((high, low), (high_ref[q], low_ref[q]))
+        mains.append(both[:, :LANES])
+        shared = both[:, LANES:] if shared is None else shared + both[:, LANES:]
+    return [*mains, shared]
+
+
+def row_product(table, tiles):
+    return quarters(product(table, split(jnp.concatenate(tiles, axis=1))))
 
 
 def collide_kernel(
-    got_ref, first_ref, second_ref, loss_ref, ph_ref, pl_ref, fh_ref, fl_ref, bh_ref, bl_ref, out_ref, x_ref, gain_ref
+    got_ref,
+    first_ref,
+    second_ref,
+    loss_ref,
+    place_ref,
+    unplace_ref,
+    gh_ref,
+    gl_ref,
+    ih_ref,
+    il_ref,
+    fh_ref,
+    fl_ref,
+    bh_ref,
+    bl_ref,
+    out_ref,
+    x_ref,
+    gain_ref,
 ):
     rows = OWN * VDIM
     for c in range(OWN):
@@ -270,30 +405,46 @@
         for m in range(4):
             tiles = [got_ref[pl.ds(m * CHUNK + t * OWN + c, 8, stride=4 * CHUNK), :] for t in range(TILES)]
             part.append(jnp.concatenate([*tiles[:3], tiles[3][:, :TAIL]], axis=1))
-        x_ref[c * VDIM : c * VDIM + 8, :] = jnp.concatenate([part[0], part[1][:, :144]], axis=1)
-        x_ref[c * VDIM + 8 : c * VDIM + 16, :] = jnp.concatenate([part[1][:, 144:], part[2][:, :288]], axis=1)
-        x_ref[c * VDIM + 16 : c * VDIM + 24, :] = jnp.concatenate([part[2][:, 288:], part[3]], axis=1)
-    plane = (ph_ref[...], pl_ref[...])
-    spectrum = product(split(x_ref[...]), plane)
-    spectrum = product((fh_ref[...], fl_ref[...]), split(spectrum))
-
-    def weighted(table):
-        return jnp.concatenate([spectrum[c * VDIM : (c + 1) * VDIM] * table for c in range(OWN)], axis=0)
-
-    back = (bh_ref[...], bl_ref[...])
-    gain_ref[...] = jnp.zeros_like(gain_ref)
+        x_ref[c * VDIM : c * VDIM + 8, :PLANE] = jnp.concatenate([part[0], part[1][:, :144]], axis=1)
+        x_ref[c * VDIM + 8 : c * VDIM + 16, :PLANE] = jnp.concatenate([part[1][:, 144:], part[2][:, :288]], axis=1)
+        x_ref[c * VDIM + 16 : c * VDIM + 24, :PLANE] = jnp.concatenate([part[2][:, 288:], part[3]], axis=1)
+    high, low = split(x_ref[:, :PLANE])
+    x_ref[...] = dot(high, place_ref[...]) + dot(low, place_ref[...])
+    tiles = quarters(x_ref[...])
+    spectrum = plane_product([*mixed(tiles[:4]), tiles[4]], gh_ref, gl_ref)
+    spectrum = row_product((fh_ref[...], fl_ref[...]), spectrum)
+
+    def weighted(tables):
+        return [
+            jnp.concatenate(
+                [
+                    spectrum[q][c * VDIM : (c + 1) * VDIM] * table[:, q * LANES : (q + 1) * LANES]
+                    for table in tables
+                    for c in range(OWN)
+                ],
+                axis=0,
+            )
+            for q in range(5)
+        ]
+
+    def image(tables, count):
+        tiles = plane_product(weighted(tables), ih_ref, il_ref)
+        tiles = row_product((bh_ref[:count, :count], bl_ref[:count, :count]), tiles)
+        return [*mixed(tiles[:4]), tiles[4]]
+
     for t in range(TERMS):
-        scaled = jnp.concatenate([weighted(first_ref[t]), weighted(second_ref[t])], axis=0)
-        image = product(back, split(product(split(scaled), plane)))
-        gain_ref[...] += image[:rows] * image[rows:]
-    image = product(
-        (bh_ref[:rows, :rows], bl_ref[:rows, :rows]), split(product(split(weighted(loss_ref[...])), plane))
-    )
-    gain_ref[...] = gain_ref[...] - x_ref[...] * image
+        both = image((first_ref[t], second_ref[t]), 2 * rows)
+        for q in range(5):
+            term = both[q][:rows] * both[q][rows:]
+            at = slice(q * LANES, (q + 1) * LANES)
+            gain_ref[:, at] = term if t == 0 else gain_ref[:, at] + term
+    lost = image((loss_ref[...],), rows)
+    high, low = split(gain_ref[...] - x_ref[...] * jnp.concatenate(lost, axis=1))
+    gain_ref[:, :PLANE] = dot(high, unplace_ref[...]) + dot(low, unplace_ref[...])
     for c in range(OWN):
-        r0 = gain_ref[c * VDIM : c * VDIM + 8, :]
-        r1 = gain_ref[c * VDIM + 8 : c * VDIM + 16, :]
-        r2 = gain_ref[c * VDIM + 16 : c * VDIM + 24, :]
+        r0 = gain_ref[c * VDIM : c * VDIM + 8, :PLANE]
+        r1 = gain_ref[c * VDIM + 8 : c * VDIM + 16, :PLANE]
+        r2 = gain_ref[c * VDIM + 16 : c * VDIM + 24, :PLANE]
         part = [
             r0[:, :WIDTH],
             jnp.concatenate([r0[:, WIDTH:], r1[:, :288]], axis=1),
@@ -345,23 +496,37 @@
     edges = shape(7 * EDGE, LANES)
     packed = shape(GROUP * CHUNK, LANES)
     change = pltpu.VMEM((TILES, CELLS, LANES), f32)
+    inner = shape(2, TILES, BSIDE, BSIDE, LANES)
+    pick = jax.ShapeDtypeStruct((ACT, CELLS), bf16)
     mask = collide_mask.reshape(1, CELLS)
-
-    cells, edge = call(pack_kernel, [], [distribution], (tiles, edges), name="pack_edges")
-    near_a, near_b = swap_edges(edge)
+    scalars = [neighbours, block_level]
+
+    cells, edge = call(pack_kernel, [], [distribution.swapaxes(1, 2)], (tiles, edges), name="pack_edges")
+    near = swap_edges(edge)
+    inside = call(inner_kernel, [], [cells], inner, name="first_inner")
     one, edge_one = call(
-        first_kernel,
-        [neighbours, block_level],
-        [cells, edge, near_a, near_b],
-        (tiles, edges),
-        [change],
-        name="first_section",
-    )
-    near_a, near_b = swap_edges(edge_one)
+        first_kernel, scalars, [cells, inside, edge, *near], (tiles, edges), [change], name="first_section"
+    )
+    near = swap_edges(edge_one)
+    inside, pick = call(inner_slots_kernel, [], [mask, one], (inner, pick), name="second_inner")
+    weights = [
+        gain_first.reshape(TERMS * VDIM, PLANE),
+        gain_second.reshape(TERMS * VDIM, PLANE),
+        loss_rates.reshape(VDIM, PLANE),
+    ]
+    tables = call(
+        order_kernel,
+        [],
+        [*weights, pieces["order"]],
+        tuple(shape(w.shape[0], WIDE) for w in weights),
+        name="order_weights",
+    )
+    tables = (*(t.reshape(TERMS, VDIM, WIDE) for t in tables[:2]), tables[2])
+    pick, tables = lax.optimization_barrier((pick, tables))
     two, send = call(
         second_kernel,
-        [neighbours, block_level],
-        [mask, cells, one, edge_one, near_a, near_b],
+        scalars,
+        [pick, cells, one, inside, edge_one, *near],
         (tiles, packed),
         [change],
         name="second_section",
@@ -372,19 +537,21 @@
         [],
         [
             got,
-            gain_first.reshape(TERMS, VDIM, PLANE),
-            gain_second.reshape(TERMS, VDIM, PLANE),
-            loss_rates.reshape(VDIM, PLANE),
-            *pieces,
+            *tables,
+            pieces["place"],
+            pieces["unplace"],
+            *pieces["plane_forward"],
+            *pieces["plane_back"],
+            *pieces["row_forward"],
+            *pieces["row_back"],
         ],
         packed,
-        [pltpu.VMEM((OWN * VDIM, PLANE), f32)] * 2,
+        [pltpu.VMEM((OWN * VDIM, WIDE), f32)] * 2,
         name="collide",
     )
     back = lax.all_to_all(collided, "vel", split_axis=0, concat_axis=0, tiled=True)
-    return call(
-        last_kernel, [], [mask, two, back], shape(1, CELLS, WIDTH), name="add_collision"
-    )
+    total = call(last_kernel, [], [pick, two, back], shape(1, WIDTH, CELLS), name="add_collision")
+    return total.swapaxes(1, 2)
 
 
 def solution(mesh):

time: 74.3 us -> 67.7 us (0.911)
  blocking collectives: 17.1 us -> 40.5 us
  waiting for transfers between devices: 22.8 us -> 2.15 us
  starting transfers between devices: 14.2 us -> 5.5 us
  local copies, waits for them, and re-layouts: 4.33 us -> 3.21 us
    all_to_all x0 -> x1, blocking collectives: none -> 22.5 us  [shards(): got = lax.all_to_all(send, 'vel', split_axis=0, concat_axis=0, tiled=True)]
    all_to_all x1 -> x0, waiting for transfers between devices: 12.1 us -> none  [shards(): got = lax.all_to_all(send, 'vel', split_axis=0, concat_axis=0, tiled=True)]
    all_to_all x1 -> x0, starting transfers between devices: 11.6 us -> none  [shards(): got = lax.all_to_all(send, 'vel', split_axis=0, concat_axis=0, tiled=True)]
    ppermute x2, waiting for transfers between devices: 9.45 us -> 2.14 us  [swap_edges(): lax.ppermute(edge, 'space', other)]
    ppermute x2, starting transfers between devices: 1.73 us -> 4.71 us  [swap_edges(): lax.ppermute(edge, 'space', pair)]
    ppermute x2, waiting for transfers between devices: 1.24 us -> 0.01 us  [swap_edges(): lax.ppermute(edge, 'space', pair)]
    pallas_call x1 -> x0, local copies, waits for them, and re-layouts: 0.94 us -> none  [call(): pl.pallas_call(kernel, out_shape=outs, in_specs=[SMALL] * len(small) + [B...]
    all_to_all x1, blocking collectives: 17.1 us -> 18 us  [shards(): lax.all_to_all(collided, 'vel', split_axis=0, concat_axis=0, tiled=True)]
  transfers between devices with their start and end apart: 5 -> 4, of which waited for: 4 -> 1; matrix products, arithmetic and copies ran while one was open for 2% -> 2% of each run, Pallas kernels for 0% -> 5%
where the time goes in v1:
time: 67.7 us; the launch traced here: 67.4 us
  blocking collectives  40.5 us (60%)
  Pallas kernels  15.1 us (22%)
  starting transfers between devices  5.5 us (8%)
  local copies, waits for them, and re-layouts  3.21 us (5%)
  waiting for transfers between devices  2.15 us (3%)
  between operations  0.91 us (1%)
    all_to_all x1, blocking collectives, shards(): got = lax.all_to_all(send, 'vel', split_axis=0, concat_axis=0, tiled=True)  22.5 us
    all_to_all x1, blocking collectives, shards(): lax.all_to_all(collided, 'vel', split_axis=0, concat_axis=0, tiled=True)  18 us
    pallas_call x8, Pallas kernels, call(): pl.pallas_call(kernel, out_shape=outs, in_specs=[SMALL] * len(small) + [B...  15.1 us
    ppermute x2, starting transfers between devices, swap_edges(): lax.ppermute(edge, 'space', pair)  4.71 us
    ppermute x2, waiting for transfers between devices, swap_edges(): lax.ppermute(edge, 'space', other)  2.14 us
    unnamed x32, local copies, waits for them, and re-layouts  1.78 us
  transfers between devices with their start and end apart: 4, of which 1 were waited for; matrix products, arithmetic and copies ran while one was open for 2% of the time, Pallas kernels for 5%

profile of v1, /device:TPU:24, one launch (start us, length us, event | category | flops | bytes accessed | tf_op | source)
XLA Modules:
  0.0 67.4 jit_solution(2243432257822050216)
XLA Ops:
  0.0 1.0 %copy-done.7 = f32[1,256,432]{1,2,0:T(8,128)S(1)} copy-done((f32[1,256,432]{1,2,0:T(8,128)S(1)}, f32[1,256,432]{1,2,0:T(8,128)}, u32[]{:S(2)}) %copy-start.7) | copy-done | bytes 442392
  1.0 0.3 pack_edges.1
  1.3 0.2 collective-permute-start.1
  1.6 1.9 %collective-permute-start = (f32[560,128]{1,0:T(8,128)S(1)}, f32[560,128]{1,0:T(8,128)S(1)}, u32[]{:S(2)}, u32[]{:S(2)}) collective-permute-start(f32[560,128]{1,0:T(8,128)S(1)} %get-tuple-element.21.own_ref), channel_id=1, source_target_pairs={{0,32},{32,0},{64,96},{96,64},{128,160},{160,128},{192,224},{224,1... | collective-permute-start | bytes 860168 | tf_op jit(solution)/shard_map/ppermute | solution.py:488
  4.1 0.0 copy-start.12
  4.1 1.2 %first_inner.1.inner_ref = f32[2,4,16,16,128]{4,3,2,1,0:T(8,128)S(1)} custom-call(f32[4,256,128]{2,1,0:T(8,128)S(1)} %get-tuple-element.20.cells_ref.x_ref.base_ref), custom_call_target="tpu_custom_call" | custom-call | tf_op jit(solution)/shard_map/first_inner/pallas_call | solution.py:473
  5.3 0.0 copy-start.15
  5.3 0.0 copy-start.14
  5.3 2.1 %collective-permute-done.1.b_ref = f32[560,128]{1,0:T(8,128)S(1)} collective-permute-done((f32[560,128]{1,0:T(8,128)S(1)}, f32[560,128]{1,0:T(8,128)S(1)}, u32[]{:S(2)}, u32[]{:S(2)}) %collective-permute-start.1) | collective-permute-done | bytes 286752 | tf_op jit(solution)/shard_map/ppermute | solution.py:488
  7.4 0.0 collective-permute-done.a_ref
  7.4 0.0 copy-done.12
  7.4 1.4 %first_section.1 = (f32[4,256,128]{2,1,0:T(8,128)S(1)}, f32[560,128]{1,0:T(8,128)S(1)}) custom-call(s32[1,4]{1,0:T(1,128)S(1)} %copy-done.12, s32[1]{0:T(128)S(6)} %copy.19.level_ref, f32[4,256,128]{2,1,0:T(8,128)S(1)} %get-tuple-element.20.cells_ref.x_ref.base_ref, f32[2,4,16,16,128]{4,3,2,1,0:T(8,128)S(1)} %first_inner.1.inner_ref, ...), custom_call_target="tpu_custom_call" | custom-call | tf_op jit(solution)/shard_map/first_section/pallas_call | solution.py:473
  8.9 0.6 collective-permute-start.3
  9.5 2.8 %collective-permute-start.2 = (f32[560,128]{1,0:T(8,128)S(1)}, f32[560,128]{1,0:T(8,128)S(1)}, u32[]{:S(2)}, u32[]{:S(2)}) collective-permute-start(f32[560,128]{1,0:T(8,128)S(1)} %get-tuple-element.29.own_ref), channel_id=1, source_target_pairs={{0,32},{32,0},{64,96},{96,64},{128,160},{160,128},{192,224},{224,1... | collective-permute-start | bytes 860168 | tf_op jit(solution)/shard_map/ppermute | solution.py:488
  12.3 0.0 copy-done.15
  12.3 0.1 reshape.25.loss_ref
  12.3 0.0 copy-done.14
  12.4 0.0 copy-start.2
  12.4 0.1 reshape.23.first_ref
  12.5 1.2 %reshape.24.second_ref = f32[144,576]{1,0:T(8,128)S(1)} reshape(f32[6,13824]{1,0:T(8,128)} %param.23) | data formatting | bytes 663552 | tf_op jit(solution)/shard_map/reshape | solution.py:514
  13.7 0.0 copy-done.2
  13.7 1.1 %order_weights.1 = (f32[144,640]{1,0:T(8,128)S(1)}, f32[144,640]{1,0:T(8,128)S(1)}, f32[24,640]{1,0:T(8,128)S(1)}) custom-call(f32[144,576]{1,0:T(8,128)S(1)} %reshape.23.first_ref, f32[144,576]{1,0:T(8,128)S(1)} %reshape.24.second_ref, f32[24,576]{1,0:T(8,128)S(1)} %reshape.25.loss_ref, bf16[576,640]{1,0:T(8,128)(2,1)S(1)} %copy-done.2), custom_call_target="tpu_custom_call" | custom-call | tf_op jit(solution)/shard_map/order_weights/pallas_call | solution.py:473
  14.8 0.0 copy-start.13
  14.8 0.7 %copy-done.13 = s32[256]{0:T(256)S(1)} copy-done((s32[256]{0:T(256)S(1)}, s32[256]{0:T(256)}, u32[]{:S(2)}) %copy-start.13) | copy-done | bytes 1048
  15.5 1.4 %second_inner.1 = (f32[2,4,16,16,128]{4,3,2,1,0:T(8,128)S(1)}, bf16[128,256]{1,0:T(8,128)(2,1)S(1)}) custom-call(s32[1,256]{1,0:T(1,128)S(1)} %bitcast.16, f32[4,256,128]{2,1,0:T(8,128)S(1)} %get-tuple-element.22.cells_ref.x_ref), custom_call_target="tpu_custom_call" | custom-call | tf_op jit(solution)/shard_map/second_inner/pallas_call | solution.py:473
  16.9 0.0 collective-permute-done.3.b_ref
  16.9 0.0 collective-permute-done.2.a_ref
  16.9 0.0 copy-start
  16.9 0.0 copy-start.1
  16.9 0.0 copy-start.4
  16.9 0.0 copy-start.5
  16.9 0.0 copy-start.8
  17.0 0.0 copy-start.9
  17.0 0.0 copy-start.10
  17.0 0.0 copy-start.11
  17.0 1.7 %second_section.1 = (f32[4,256,128]{2,1,0:T(8,128)S(1)}, f32[512,128]{1,0:T(8,128)S(1)}) custom-call(s32[1,4]{1,0:T(1,128)S(1)} %copy-done.12, s32[1]{0:T(128)S(6)} %copy.19.level_ref, bf16[128,256]{1,0:T(8,128)(2,1)S(1)} %get-tuple-element.27.pick_ref, f32[4,256,128]{2,1,0:T(8,128)S(1)} %get-tuple-element.20.cells_ref.x_ref.base_ref, ...), custom_call_target="tpu_custom_call" | custom-call | tf_op jit(solution)/shard_map/second_section/pallas_call | solution.py:473
  18.7 0.0 copy-start.3
  18.7 22.5 %all_to_all.22 = f32[32,16,128]{2,1,0:T(8,128)S(1)} all-to-all(f32[32,16,128]{2,1,0:T(8,128)S(1)} %bitcast.15), channel_id=1, replica_groups=mesh['space'=8,'vel'=32] {'vel'}, dimensions={0} | all-to-all | bytes 524288 | tf_op jit(solution)/shard_map/all_to_all | solution.py:534
  41.3 0.0 copy-done.6
  41.3 0.0 copy-done
  41.3 0.0 copy-done.1
  41.3 0.0 copy-done.4
  41.3 0.0 copy-done.5
  41.3 0.0 copy-done.8
  41.3 0.0 copy-done.9
  41.3 6.8 %collide.1 = f32[512,128]{1,0:T(8,128)S(1)} custom-call(f32[512,128]{1,0:T(8,128)S(1)} %bitcast.9, f32[6,24,640]{2,1,0:T(8,128)S(1)} %bitcast.13, f32[6,24,640]{2,1,0:T(8,128)S(1)} %bitcast.14, f32[24,640]{1,0:T(8,128)S(1)} %get-tuple-element.34.loss_ref, bf16[576,640]{1,0:T(8,128)(2,1)S(1)} %copy-done.1, bf16[640,576]{1,0:T(8,128)(2,1)S(1)} %copy-done, ...), custom_call_target="tpu_custom_call" | custom-call | tf_op jit(solution)/shard_map/collide/pallas_call | solution.py:473
  48.1 18.0 %all_to_all.23 = f32[32,16,128]{2,1,0:T(8,128)S(1)} all-to-all(f32[32,16,128]{2,1,0:T(8,128)S(1)} %bitcast.10), channel_id=1, replica_groups=mesh['space'=8,'vel'=32] {'vel'}, dimensions={0} | all-to-all | bytes 524288 | tf_op jit(solution)/shard_map/all_to_all | solution.py:552
  66.2 1.3 %add_collision.1 = f32[1,432,256]{2,1,0:T(8,128)} custom-call(bf16[128,256]{1,0:T(8,128)(2,1)S(1)} %get-tuple-element.27.pick_ref, f32[4,256,128]{2,1,0:T(8,128)S(1)} %get-tuple-element.30.cells_ref, f32[512,128]{1,0:T(8,128)S(1)} %bitcast.11), custom_call_target="tpu_custom_call" | custom-call | tf_op jit(solution)/shard_map/add_collision/pallas_call | solution.py:473
  (5 shorter events, 0.0 us)
Async XLA Ops:
  0.0 1.0 %copy-start.7 = (f32[1,256,432]{1,2,0:T(8,128)S(1)}, f32[1,256,432]{1,2,0:T(8,128)}, u32[]{:S(2)}) copy-start(f32[1,256,432]{1,2,0:T(8,128)} %param.18) | copy-start | bytes 1327108
  1.3 6.1 %collective-permute-start.1 = (f32[560,128]{1,0:T(8,128)S(1)}, f32[560,128]{1,0:T(8,128)S(1)}, u32[]{:S(2)}, u32[]{:S(2)}) collective-permute-start(f32[560,128]{1,0:T(8,128)S(1)} %get-tuple-element.21.own_ref), channel_id=1, source_target_pairs={{0,224},{32,64},{64,32},{96,128},{128,96},{160,192},{192,160},{224... | collective-permute-start | bytes 860168 | tf_op jit(solution)/shard_map/ppermute | solution.py:488
  1.6 5.9 %collective-permute-start = (f32[560,128]{1,0:T(8,128)S(1)}, f32[560,128]{1,0:T(8,128)S(1)}, u32[]{:S(2)}, u32[]{:S(2)}) collective-permute-start(f32[560,128]{1,0:T(8,128)S(1)} %get-tuple-element.21.own_ref), channel_id=1, source_target_pairs={{0,32},{32,0},{64,96},{96,64},{128,160},{160,128},{192,224},{224,1... | collective-permute-start | bytes 860168 | tf_op jit(solution)/shard_map/ppermute | solution.py:488
  4.1 3.3 %copy-start.12 = (s32[1,4]{1,0:T(1,128)S(1)}, s32[1,4]{1,0:T(1,128)}, u32[]{:S(2)}) copy-start(s32[1,4]{1,0:T(1,128)} %near_ref.3) | copy-start | bytes 52
  5.3 7.0 %copy-start.15 = (f32[13824]{0:T(1024)S(1)}, f32[13824]{0:T(1024)}, u32[]{:S(2)}) copy-start(f32[13824]{0:T(1024)} %param.24) | copy-start | bytes 165892
  5.3 7.1 %copy-start.14 = (f32[6,13824]{1,0:T(8,128)S(1)}, f32[6,13824]{1,0:T(8,128)}, u32[]{:S(2)}) copy-start(f32[6,13824]{1,0:T(8,128)} %param.22) | copy-start | bytes 995332
  8.9 8.0 %collective-permute-start.3 = (f32[560,128]{1,0:T(8,128)S(1)}, f32[560,128]{1,0:T(8,128)S(1)}, u32[]{:S(2)}, u32[]{:S(2)}) collective-permute-start(f32[560,128]{1,0:T(8,128)S(1)} %get-tuple-element.29.own_ref), channel_id=1, source_target_pairs={{0,224},{32,64},{64,32},{96,128},{128,96},{160,192},{192,160},{224... | collective-permute-start | bytes 860168 | tf_op jit(solution)/shard_map/ppermute | solution.py:488
  9.5 7.4 %collective-permute-start.2 = (f32[560,128]{1,0:T(8,128)S(1)}, f32[560,128]{1,0:T(8,128)S(1)}, u32[]{:S(2)}, u32[]{:S(2)}) collective-permute-start(f32[560,128]{1,0:T(8,128)S(1)} %get-tuple-element.29.own_ref), channel_id=1, source_target_pairs={{0,32},{32,0},{64,96},{96,64},{128,160},{160,128},{192,224},{224,1... | collective-permute-start | bytes 860168 | tf_op jit(solution)/shard_map/ppermute | solution.py:488
  12.4 1.4 %copy-start.2 = (bf16[576,640]{1,0:T(8,128)(2,1)S(1)}, bf16[576,640]{1,0:T(8,128)(2,1)}, u32[]{:S(2)}) copy-start(bf16[576,640]{1,0:T(8,128)(2,1)} %constant.24.clone.order_ref) | copy-start | bytes 2211844
  14.8 0.7 %copy-start.13 = (s32[256]{0:T(256)S(1)}, s32[256]{0:T(256)}, u32[]{:S(2)}) copy-start(s32[256]{0:T(256)} %param.21) | copy-start | bytes 3076
  15.5 25.8 %copy-start.6 = (bf16[4,256,256]{2,1,0:T(8,128)(2,1)S(1)}, bf16[4,256,256]{2,1,0:T(8,128)(2,1)}, u32[]{:S(2)}) copy-start(bf16[4,256,256]{2,1,0:T(8,128)(2,1)} %constant.25.clone.gh_ref) | copy-start | bytes 1572868
  16.9 24.4 %copy-start = (bf16[640,576]{1,0:T(8,128)(2,1)S(1)}, bf16[640,576]{1,0:T(8,128)(2,1)}, u32[]{:S(2)}) copy-start(bf16[640,576]{1,0:T(8,128)(2,1)} %constant.23.clone.unplace_ref) | copy-start | bytes 2211844
  16.9 24.4 %copy-start.1 = (bf16[576,640]{1,0:T(8,128)(2,1)S(1)}, bf16[576,640]{1,0:T(8,128)(2,1)}, u32[]{:S(2)}) copy-start(bf16[576,640]{1,0:T(8,128)(2,1)} %constant.22.clone.place_ref) | copy-start | bytes 2211844
  16.9 24.3 %copy-start.4 = (bf16[4,256,256]{2,1,0:T(8,128)(2,1)S(1)}, bf16[4,256,256]{2,1,0:T(8,128)(2,1)}, u32[]{:S(2)}) copy-start(bf16[4,256,256]{2,1,0:T(8,128)(2,1)} %constant.27.clone.ih_ref) | copy-start | bytes 1572868
  16.9 24.3 %copy-start.5 = (bf16[4,256,256]{2,1,0:T(8,128)(2,1)S(1)}, bf16[4,256,256]{2,1,0:T(8,128)(2,1)}, u32[]{:S(2)}) copy-start(bf16[4,256,256]{2,1,0:T(8,128)(2,1)} %constant.26.clone.gl_ref) | copy-start | bytes 1572868
  16.9 24.3 %copy-start.8 = (bf16[192,192]{1,0:T(8,128)(2,1)S(1)}, bf16[192,192]{1,0:T(8,128)(2,1)}, u32[]{:S(2)}) copy-start(bf16[192,192]{1,0:T(8,128)(2,1)} %constant.32.clone.bl_ref) | copy-start | bytes 221188
  17.0 24.3 %copy-start.9 = (bf16[192,192]{1,0:T(8,128)(2,1)S(1)}, bf16[192,192]{1,0:T(8,128)(2,1)}, u32[]{:S(2)}) copy-start(bf16[192,192]{1,0:T(8,128)(2,1)} %constant.31.clone.bh_ref) | copy-start | bytes 221188
  17.0 24.3 %copy-start.10 = (bf16[96,96]{1,0:T(8,128)(2,1)S(1)}, bf16[96,96]{1,0:T(8,128)(2,1)}, u32[]{:S(2)}) copy-start(bf16[96,96]{1,0:T(8,128)(2,1)} %constant.30.clone.fl_ref) | copy-start | bytes 55300
  17.0 24.3 %copy-start.11 = (bf16[96,96]{1,0:T(8,128)(2,1)S(1)}, bf16[96,96]{1,0:T(8,128)(2,1)}, u32[]{:S(2)}) copy-start(bf16[96,96]{1,0:T(8,128)(2,1)} %constant.29.clone.fh_ref) | copy-start | bytes 55300
  18.7 22.6 %copy-start.3 = (bf16[4,256,256]{2,1,0:T(8,128)(2,1)S(1)}, bf16[4,256,256]{2,1,0:T(8,128)(2,1)}, u32[]{:S(2)}) copy-start(bf16[4,256,256]{2,1,0:T(8,128)(2,1)} %constant.28.clone.il_ref) | copy-start | bytes 1572868

commit v2 on v1

--- a/solution.py
+++ b/solution.py
@@ -41,8 +41,6 @@
     k = np.arange(VDIM)
     angle = 2.0 * np.pi * ((k[:, None] * k[None, :]) % VDIM) / VDIM
     table = (np.cos(angle) + np.sin(angle)) / np.sqrt(VDIM)
-    place = np.arange(VDIM)
-    first = 3 * (place % 8) + place // 8
 
     def pieces(array):
         high = array.astype(ml_dtypes.bfloat16)
@@ -54,8 +52,10 @@
     physical[
         np.arange(PLANE), quarter_lane(2 * (j // HALF) + c // HALF, (j % HALF) * HALF + c % HALF)
     ] = 1.0
-    spectral = np.zeros((PLANE, WIDE))
-    spectral[np.arange(PLANE), quarter_lane(2 * (j % 2) + c % 2, (j // 2) * HALF + c // 2)] = 1.0
+    spectral = np.zeros((2, WIDE, WIDE))
+    for odd in range(2):
+        skip = odd * (LANES // 2)
+        spectral[odd, skip + np.arange(PLANE), quarter_lane(2 * (j % 2) + c % 2, (j // 2) * HALF + c // 2)] = 1.0
 
     blocks = np.zeros((4, 2 * LANES, 2 * LANES))
     spot = np.arange(QUARTER)
@@ -68,16 +68,13 @@
             jh, kh = divmod(g, 2)
             row = LANES + 16 * g + np.arange(QUARTER - LANES)
             blocks[q][np.ix_(row, column)] = (-1.0) ** (jh * jp + kh * kp) * block[LANES:]
-    forward = np.kron(np.eye(OWN), table[:, first])
-    back = np.kron(np.eye(2 * OWN), table[first, :])
+    blocks = blocks / np.sqrt(VDIM)
     return dict(
         place=jnp.asarray(physical.astype(ml_dtypes.bfloat16)),
         unplace=jnp.asarray(physical.T.astype(ml_dtypes.bfloat16)),
-        order=jnp.asarray(spectral.astype(ml_dtypes.bfloat16)),
+        order=[jnp.asarray(o.astype(ml_dtypes.bfloat16)) for o in spectral],
         plane_forward=pieces(blocks),
         plane_back=pieces(blocks.transpose(0, 2, 1)),
-        row_forward=pieces(forward),
-        row_back=pieces(back),
     )
 
 
@@ -347,11 +344,23 @@
             out_ref[0, tile * LANES : tile * LANES + wide, :] = total.T[:wide]
 
 
-def order_kernel(first_ref, second_ref, loss_ref, order_ref, first_out, second_out, loss_out):
-    order = order_ref[...]
-    for table, out in ((first_ref, first_out), (second_ref, second_out), (loss_ref, loss_out)):
-        high, low = split(table[...])
-        out[...] = dot(high, order) + dot(low, order)
+def order_kernel(first_ref, second_ref, loss_ref, even_ref, odd_ref, out_one, out_two, one_ref, two_ref):
+    order = (even_ref[...], odd_ref[...])
+    for i in range(VDIM):
+        start = i * PLANE - (i % 2) * (LANES // 2)
+        window = slice(start, start + WIDE)
+        at = i // 2 + (i % 2) * HALF
+        one_ref[at, :TERMS, :] = first_ref[:, window]
+        one_ref[at, TERMS : TERMS + 1, :] = loss_ref[:, window]
+        one_ref[at, TERMS + 1 :, :] = jnp.zeros((7 - TERMS, WIDE), f32)
+        two_ref[at, :TERMS, :] = second_ref[:, window]
+        two_ref[at, TERMS:, :] = jnp.zeros((8 - TERMS, WIDE), f32)
+    for source, out in ((one_ref, out_one), (two_ref, out_two)):
+        for odd in range(2):
+            high, low = split(source[odd * HALF : (odd + 1) * HALF].reshape(HALF * 8, WIDE))
+            table = dot(high, order[odd]) + dot(low, order[odd])
+            for m in range(HALF):
+                out[2 * m + odd] = table[8 * m : 8 * m + 8]
 
 
 def quarters(wide):
@@ -376,75 +385,152 @@
     return [*mains, shared]
 
 
-def row_product(table, tiles):
-    return quarters(product(table, split(jnp.concatenate(tiles, axis=1))))
+COS15, COS30, COS45, COS75 = (float(np.cos(np.pi * a / 180.0)) for a in (15, 30, 45, 75))
+
+
+def row_transform(x):
+    e = {j: x[j] + x[24 - j] for j in range(1, 12)}
+    o = {j: x[j] - x[24 - j] for j in range(1, 12)}
+    c, s = {}, {}
+
+    u = x[0] + x[12]
+    a = {j: e[j] + e[12 - j] for j in range(1, 6)}
+    p0, p1, p2, p3 = u + e[6], a[1] + a[5], a[2] + a[4], a[3]
+    g, h, m, n = p0 + p3, p0 - p3, p1 + p2, p1 - p2
+    c[0], c[4], c[8], c[12] = g + m, h + 0.5 * n, g - 0.5 * m, h - n
+    q0, q1, q2 = u - e[6], COS30 * (a[1] - a[5]), a[2] - a[4]
+    w = q0 + 0.5 * q2
+    c[2], c[6], c[10] = w + q1, q0 - q2, w - q1
+    v = x[0] - x[12]
+    b = {j: e[j] - e[12 - j] for j in range(1, 6)}
+    w, z = v + 0.5 * b[4], COS30 * b[2]
+    even = {1: w + z, 3: v - b[4], 5: w - z}
+    t = COS45 * b[3]
+    odd = {
+        1: COS15 * b[1] + t + COS75 * b[5],
+        3: COS45 * (b[1] - b[3] - b[5]),
+        5: COS75 * b[1] - t + COS15 * b[5],
+    }
+    for k in (1, 3, 5):
+        c[k], c[12 - k] = even[k] + odd[k], even[k] - odd[k]
+    a = {j: o[j] + o[12 - j] for j in range(1, 6)}
+    w, z = 0.5 * a[2] + o[6], COS30 * a[4]
+    even = {1: w + z, 3: a[2] - o[6], 5: w - z}
+    t = COS45 * a[3]
+    odd = {
+        1: COS75 * a[1] + t + COS15 * a[5],
+        3: COS45 * (a[1] + a[3] - a[5]),
+        5: COS15 * a[1] - t + COS75 * a[5],
+    }
+    for k in (1, 3, 5):
+        s[k], s[12 - k] = odd[k] + even[k], odd[k] - even[k]
+    b = {j: o[j] - o[12 - j] for j in range(1, 6)}
+    p1, p2 = b[1] + b[5], COS30 * (b[2] + b[4])
+    w = 0.5 * p1 + b[3]
+    s[2], s[6], s[10] = w + p2, p1 - b[3], w - p2
+    p1, p2 = COS30 * (b[1] - b[5]), COS30 * (b[2] - b[4])
+    s[4], s[8] = p1 + p2, p1 - p2
+
+    out = [None] * 24
+    out[0], out[12] = c[0], c[12]
+    for k in range(1, 12):
+        out[k], out[24 - k] = c[k] + s[k], c[k] - s[k]
+    return out
+
+
+def transform_rows(tiles, out_ref):
+    for q in range(5):
+        out = row_transform([tiles[q][8 * i : 8 * i + 8] for i in range(VDIM)])
+        for i in range(VDIM):
+            out_ref[q, 8 * i : 8 * i + 8, :] = out[i]
+
+
+def row_image(ref, i):
+    tiles = [ref[q, 8 * i : 8 * i + 8, :] for q in range(5)]
+    return [*mixed(tiles[:4]), tiles[4]]
 
 
 def collide_kernel(
     got_ref,
-    first_ref,
-    second_ref,
-    loss_ref,
+    one_ref,
+    two_ref,
     place_ref,
     unplace_ref,
     gh_ref,
     gl_ref,
     ih_ref,
     il_ref,
-    fh_ref,
-    fl_ref,
-    bh_ref,
-    bl_ref,
     out_ref,
+    flat_ref,
     x_ref,
-    gain_ref,
+    spectrum_ref,
+    first_ref,
+    second_ref,
+    total_ref,
 ):
-    rows = OWN * VDIM
     for c in range(OWN):
         part = []
         for m in range(4):
             tiles = [got_ref[pl.ds(m * CHUNK + t * OWN + c, 8, stride=4 * CHUNK), :] for t in range(TILES)]
             part.append(jnp.concatenate([*tiles[:3], tiles[3][:, :TAIL]], axis=1))
-        x_ref[c * VDIM : c * VDIM + 8, :PLANE] = jnp.concatenate([part[0], part[1][:, :144]], axis=1)
-        x_ref[c * VDIM + 8 : c * VDIM + 16, :PLANE] = jnp.concatenate([part[1][:, 144:], part[2][:, :288]], axis=1)
-        x_ref[c * VDIM + 16 : c * VDIM + 24, :PLANE] = jnp.concatenate([part[2][:, 288:], part[3]], axis=1)
-    high, low = split(x_ref[:, :PLANE])
-    x_ref[...] = dot(high, place_ref[...]) + dot(low, place_ref[...])
-    tiles = quarters(x_ref[...])
-    spectrum = plane_product([*mixed(tiles[:4]), tiles[4]], gh_ref, gl_ref)
-    spectrum = row_product((fh_ref[...], fl_ref[...]), spectrum)
-
-    def weighted(tables):
-        return [
-            jnp.concatenate(
-                [
-                    spectrum[q][c * VDIM : (c + 1) * VDIM] * table[:, q * LANES : (q + 1) * LANES]
-                    for table in tables
-                    for c in range(OWN)
-                ],
-                axis=0,
-            )
-            for q in range(5)
-        ]
-
-    def image(tables, count):
-        tiles = plane_product(weighted(tables), ih_ref, il_ref)
-        tiles = row_product((bh_ref[:count, :count], bl_ref[:count, :count]), tiles)
-        return [*mixed(tiles[:4]), tiles[4]]
-
-    for t in range(TERMS):
-        both = image((first_ref[t], second_ref[t]), 2 * rows)
+        flat_ref[c * VDIM : c * VDIM + 8, :] = jnp.concatenate([part[0], part[1][:, :144]], axis=1)
+        flat_ref[c * VDIM + 8 : c * VDIM + 16, :] = jnp.concatenate([part[1][:, 144:], part[2][:, :288]], axis=1)
+        flat_ref[c * VDIM + 16 : c * VDIM + 24, :] = jnp.concatenate([part[2][:, 288:], part[3]], axis=1)
+    high, low = split(flat_ref[...])
+    placed = dot(high, place_ref[...]) + dot(low, place_ref[...])
+    for c in range(OWN):
+        for r in range(3):
+            for q in range(5):
+                value = placed[c * VDIM + 8 * r : c * VDIM + 8 * r + 8, q * LANES : (q + 1) * LANES]
+                for copy in (0, OWN):
+                    x_ref[q, pl.ds(8 * r + c + copy, 8, stride=VDIM), :] = value
+    tiles = [x_ref[q] for q in range(5)]
+    transform_rows(plane_product([*mixed(tiles[:4]), tiles[4]], gh_ref, gl_ref), spectrum_ref)
+
+    upper = lax.broadcasted_iota(jnp.int32, (8, LANES), 0) < OWN
+
+    def repeated(table_ref, i, t, q):
+        return jnp.broadcast_to(table_ref[i, t : t + 1, q * LANES : (q + 1) * LANES], (8, LANES))
+
+    def image(table_ref, top, bottom, out_ref):
+        tiles = []
         for q in range(5):
-            term = both[q][:rows] * both[q][rows:]
-            at = slice(q * LANES, (q + 1) * LANES)
-            gain_ref[:, at] = term if t == 0 else gain_ref[:, at] + term
-    lost = image((loss_ref[...],), rows)
-    high, low = split(gain_ref[...] - x_ref[...] * jnp.concatenate(lost, axis=1))
-    gain_ref[:, :PLANE] = dot(high, unplace_ref[...]) + dot(low, unplace_ref[...])
+            pieces = []
+            for i in range(VDIM):
+                table = repeated(table_ref, i, top, q)
+                if bottom != top:
+                    table = jnp.where(upper, table, repeated(table_ref, i, bottom, q))
+                pieces.append(spectrum_ref[q, 8 * i : 8 * i + 8, :] * table)
+            tiles.append(jnp.concatenate(pieces, axis=0))
+        transform_rows(plane_product(tiles, ih_ref, il_ref), out_ref)
+
+    for u in range(TERMS // 2):
+        image(one_ref, 2 * u, 2 * u + 1, first_ref)
+        image(two_ref, 2 * u, 2 * u + 1, second_ref)
+        for i in range(VDIM):
+            one, two = row_image(first_ref, i), row_image(second_ref, i)
+            for q in range(5):
+                at = slice(8 * i, 8 * i + 8)
+                term = one[q] * two[q]
+                total_ref[q, at, :] = term if u == 0 else total_ref[q, at, :] + term
+    image(one_ref, TERMS, TERMS, first_ref)
+    for i in range(VDIM):
+        lost = row_image(first_ref, i)
+        for q in range(5):
+            at = slice(8 * i, 8 * i + 8)
+            both = total_ref[q, at, :]
+            total_ref[q, at, :] = both + pltpu.roll(both, OWN, 0) - x_ref[q, at, :] * lost[q]
+    rows = [
+        jnp.concatenate([total_ref[q, pl.ds(8 * r + c, 8, stride=VDIM), :] for q in range(5)], axis=1)
+        for c in range(OWN)
+        for r in range(3)
+    ]
+    high, low = split(jnp.concatenate(rows, axis=0))
+    flat_ref[...] = dot(high, unplace_ref[...]) + dot(low, unplace_ref[...])
     for c in range(OWN):
-        r0 = gain_ref[c * VDIM : c * VDIM + 8, :PLANE]
-        r1 = gain_ref[c * VDIM + 8 : c * VDIM + 16, :PLANE]
-        r2 = gain_ref[c * VDIM + 16 : c * VDIM + 24, :PLANE]
+        r0 = flat_ref[c * VDIM : c * VDIM + 8, :]
+        r1 = flat_ref[c * VDIM + 8 : c * VDIM + 16, :]
+        r2 = flat_ref[c * VDIM + 16 : c * VDIM + 24, :]
         part = [
             r0[:, :WIDTH],
             jnp.concatenate([r0[:, WIDTH:], r1[:, :288]], axis=1),
@@ -500,29 +586,28 @@
     pick = jax.ShapeDtypeStruct((ACT, CELLS), bf16)
     mask = collide_mask.reshape(1, CELLS)
     scalars = [neighbours, block_level]
+    rows = (5, VDIM * 2 * OWN, LANES)
 
     cells, edge = call(pack_kernel, [], [distribution.swapaxes(1, 2)], (tiles, edges), name="pack_edges")
     near = swap_edges(edge)
-    inside = call(inner_kernel, [], [cells], inner, name="first_inner")
+    inside, pick = call(inner_slots_kernel, [], [mask, cells], (inner, pick), name="first_inner")
+    loss = loss_rates.reshape(1, -1)
+    inside, loss = lax.optimization_barrier((inside, loss))
     one, edge_one = call(
         first_kernel, scalars, [cells, inside, edge, *near], (tiles, edges), [change], name="first_section"
     )
     near = swap_edges(edge_one)
-    inside, pick = call(inner_slots_kernel, [], [mask, one], (inner, pick), name="second_inner")
-    weights = [
-        gain_first.reshape(TERMS * VDIM, PLANE),
-        gain_second.reshape(TERMS * VDIM, PLANE),
-        loss_rates.reshape(VDIM, PLANE),
-    ]
+    inside = call(inner_kernel, [], [one], inner, name="second_inner")
+    table = (VDIM, 8, WIDE)
     tables = call(
         order_kernel,
         [],
-        [*weights, pieces["order"]],
-        tuple(shape(w.shape[0], WIDE) for w in weights),
+        [gain_first, gain_second, loss, *pieces["order"]],
+        (shape(*table), shape(*table)),
+        [pltpu.VMEM(table, f32)] * 2,
         name="order_weights",
     )
-    tables = (*(t.reshape(TERMS, VDIM, WIDE) for t in tables[:2]), tables[2])
-    pick, tables = lax.optimization_barrier((pick, tables))
+    inside, tables = lax.optimization_barrier((inside, tables))
     two, send = call(
         second_kernel,
         scalars,
@@ -542,11 +627,9 @@
             pieces["unplace"],
             *pieces["plane_forward"],
             *pieces["plane_back"],
-            *pieces["row_forward"],
-            *pieces["row_back"],
         ],
         packed,
-        [pltpu.VMEM((OWN * VDIM, WIDE), f32)] * 2,
+        [pltpu.VMEM((OWN * VDIM, PLANE), f32)] + [pltpu.VMEM(rows, f32)] * 5,
         name="collide",
     )
     back = lax.all_to_all(collided, "vel", split_axis=0, concat_axis=0, tiled=True)

time: 67.7 us -> 65 us (0.960)
  Pallas kernels: 15.1 us -> 13 us
  blocking collectives: 40.5 us -> 42.3 us
  local copies, waits for them, and re-layouts: 3.21 us -> 1.79 us
  waiting for transfers between devices: 2.15 us -> 1.42 us
    pallas_call x8, Pallas kernels: 15.1 us -> 13 us  [call(): pl.pallas_call(kernel, out_shape=outs, in_specs=[SMALL] * len(small) + [B...]
    all_to_all x1, blocking collectives: 22.5 us -> 24.1 us  [shards(): got = lax.all_to_all(send, 'vel', split_axis=0, concat_axis=0, tiled=True)]
    reshape x3 -> x1, local copies, waits for them, and re-layouts: 1.42 us -> 0.04 us  [shards(): loss = loss_rates.reshape(1, -1)]
    ppermute x2, waiting for transfers between devices: 2.14 us -> 1.41 us  [swap_edges(): lax.ppermute(edge, 'space', other)]
    unnamed x32 -> x28, local copies, waits for them, and re-layouts: 1.78 us -> 1.75 us
  transfers between devices with their start and end apart: 4 -> 4, of which waited for: 1 -> 2; matrix products, arithmetic and copies ran while one was open for 2% -> 0% of each run, Pallas kernels for 5% -> 6%
where the time goes in v2:
time: 65 us; the launch traced here: 64.8 us
  blocking collectives  42.3 us (65%)
  Pallas kernels  13 us (20%)
  starting transfers between devices  5.5 us (8%)
  local copies, waits for them, and re-layouts  1.79 us (3%)
  waiting for transfers between devices  1.42 us (2%)
  between operations  0.81 us (1%)
    all_to_all x1, blocking collectives, shards(): got = lax.all_to_all(send, 'vel', split_axis=0, concat_axis=0, tiled=True)  24.1 us
    all_to_all x1, blocking collectives, shards(): lax.all_to_all(collided, 'vel', split_axis=0, concat_axis=0, tiled=True)  18.2 us
    pallas_call x8, Pallas kernels, call(): pl.pallas_call(kernel, out_shape=outs, in_specs=[SMALL] * len(small) + [B...  13 us
    ppermute x2, starting transfers between devices, swap_edges(): lax.ppermute(edge, 'space', pair)  4.71 us
    unnamed x28, local copies, waits for them, and re-layouts  1.75 us
    ppermute x2, waiting for transfers between devices, swap_edges(): lax.ppermute(edge, 'space', other)  1.41 us
  transfers between devices with their start and end apart: 4, of which 2 were waited for; matrix products, arithmetic and copies ran while one was open for 0% of the time, Pallas kernels for 6%

profile of v2, /device:TPU:24, one launch (start us, length us, event | category | flops | bytes accessed | tf_op | source)
XLA Modules:
  0.0 64.8 jit_solution(1953267361000405634)
XLA Ops:
  0.0 0.0 copy-start.8
  0.0 1.0 %copy-done.8 = f32[1,256,432]{1,2,0:T(8,128)S(1)} copy-done((f32[1,256,432]{1,2,0:T(8,128)S(1)}, f32[1,256,432]{1,2,0:T(8,128)}, u32[]{:S(2)}) %copy-start.8) | copy-done | bytes 442392
  1.0 0.0 copy-start.13
  1.0 0.3 pack_edges.1
  1.3 0.2 collective-permute-start.1
  1.6 1.9 %collective-permute-start = (f32[560,128]{1,0:T(8,128)S(1)}, f32[560,128]{1,0:T(8,128)S(1)}, u32[]{:S(2)}, u32[]{:S(2)}) collective-permute-start(f32[560,128]{1,0:T(8,128)S(1)} %get-tuple-element.24.own_ref), channel_id=1, source_target_pairs={{0,32},{32,0},{64,96},{96,64},{128,160},{160,128},{192,224},{224,1... | collective-permute-start | bytes 860168 | tf_op jit(solution)/shard_map/ppermute | solution.py:574
  4.1 0.0 copy-done.13
  4.2 0.0 copy-start.12
  4.2 0.7 %copy-done.12 = s32[256]{0:T(256)S(1)} copy-done((s32[256]{0:T(256)S(1)}, s32[256]{0:T(256)}, u32[]{:S(2)}) %copy-start.12) | copy-done | bytes 1048
  4.8 0.0 copy-start.10
  4.8 1.4 %first_inner.1 = (f32[2,4,16,16,128]{4,3,2,1,0:T(8,128)S(1)}, bf16[128,256]{1,0:T(8,128)(2,1)S(1)}) custom-call(s32[1,256]{1,0:T(1,128)S(1)} %bitcast.12, f32[4,256,128]{2,1,0:T(8,128)S(1)} %get-tuple-element.20.cells_ref.x_ref.base_ref), custom_call_target="tpu_custom_call" | custom-call | tf_op jit(solution)/shard_map/first_inner/pallas_call | solution.py:559
  6.2 0.0 copy-start.11
  6.2 0.0 copy-start.1
  6.2 0.0 copy-start.2
  6.3 0.0 copy-start.9
  6.3 1.2 %collective-permute-done.1.b_ref = f32[560,128]{1,0:T(8,128)S(1)} collective-permute-done((f32[560,128]{1,0:T(8,128)S(1)}, f32[560,128]{1,0:T(8,128)S(1)}, u32[]{:S(2)}, u32[]{:S(2)}) %collective-permute-start.1) | collective-permute-done | bytes 286752 | tf_op jit(solution)/shard_map/ppermute | solution.py:574
  7.4 0.0 collective-permute-done.a_ref
  7.4 0.0 copy-done.11
  7.4 1.5 %first_section.1 = (f32[4,256,128]{2,1,0:T(8,128)S(1)}, f32[560,128]{1,0:T(8,128)S(1)}) custom-call(s32[1,4]{1,0:T(1,128)S(1)} %copy-done.11, s32[1]{0:T(128)S(6)} %copy.16.level_ref, f32[4,256,128]{2,1,0:T(8,128)S(1)} %get-tuple-element.20.cells_ref.x_ref.base_ref, f32[2,4,16,16,128]{4,3,2,1,0:T(8,128)S(1)} %get-tuple-element.23.inner_ref, ...), custom_call_target="tpu_custom_call" | custom-call | tf_op jit(solution)/shard_map/first_section/pallas_call | solution.py:559
  8.9 0.5 collective-permute-start.3
  9.5 2.8 %collective-permute-start.2 = (f32[560,128]{1,0:T(8,128)S(1)}, f32[560,128]{1,0:T(8,128)S(1)}, u32[]{:S(2)}, u32[]{:S(2)}) collective-permute-start(f32[560,128]{1,0:T(8,128)S(1)} %get-tuple-element.30.own_ref), channel_id=1, source_target_pairs={{0,32},{32,0},{64,96},{96,64},{128,160},{160,128},{192,224},{224,1... | collective-permute-start | bytes 860168 | tf_op jit(solution)/shard_map/ppermute | solution.py:574
  12.3 0.0 copy-done.10
  12.3 0.0 copy-done.1
  12.3 0.0 copy-done.2
  12.3 0.0 copy-done.9
  12.3 1.3 %order_weights.1 = (f32[24,8,640]{2,1,0:T(8,128)S(1)}, f32[24,8,640]{2,1,0:T(8,128)S(1)}) custom-call(f32[6,13824]{1,0:T(8,128)S(1)} %copy-done.9, f32[6,13824]{1,0:T(8,128)S(1)} %copy-done.10, f32[1,13824]{1,0:T(1,128)S(1)} %reshape.11.loss_ref, bf16[640,640]{1,0:T(8,128)(2,1)S(1)} %copy-done.2, bf16[640,640]{1,0:T(8,128)(2,1)S(1)} %copy-done.1), custom_call_target="tpu_custom_call" | custom-call | tf_op jit(solution)/shard_map/order_weights/pallas_call | solution.py:559
  13.6 0.0 copy-start.7
  13.7 1.2 %second_inner.1.inner_ref = f32[2,4,16,16,128]{4,3,2,1,0:T(8,128)S(1)} custom-call(f32[4,256,128]{2,1,0:T(8,128)S(1)} %get-tuple-element.25.cells_ref.x_ref), custom_call_target="tpu_custom_call" | custom-call | tf_op jit(solution)/shard_map/second_inner/pallas_call | solution.py:559
  14.8 0.2 collective-permute-done.3.b_ref
  15.1 0.0 collective-permute-done.2.a_ref
  15.1 0.0 copy-start
  15.1 0.0 copy-start.3
  15.1 0.0 copy-start.5
  15.1 0.0 copy-start.6
  15.1 1.7 %second_section.1 = (f32[4,256,128]{2,1,0:T(8,128)S(1)}, f32[512,128]{1,0:T(8,128)S(1)}) custom-call(s32[1,4]{1,0:T(1,128)S(1)} %copy-done.11, s32[1]{0:T(128)S(6)} %copy.16.level_ref, bf16[128,256]{1,0:T(8,128)(2,1)S(1)} %get-tuple-element.21.pick_ref, f32[4,256,128]{2,1,0:T(8,128)S(1)} %get-tuple-element.20.cells_ref.x_ref.base_ref, ...), custom_call_target="tpu_custom_call" | custom-call | tf_op jit(solution)/shard_map/second_section/pallas_call | solution.py:559
  16.8 0.0 copy-start.4
  16.8 24.1 %all_to_all.22 = f32[32,16,128]{2,1,0:T(8,128)S(1)} all-to-all(f32[32,16,128]{2,1,0:T(8,128)S(1)} %bitcast.11), channel_id=1, replica_groups=mesh['space'=8,'vel'=32] {'vel'}, dimensions={0} | all-to-all | bytes 524288 | tf_op jit(solution)/shard_map/all_to_all | solution.py:619
  40.9 0.0 copy-done.7
  40.9 0.0 copy-done
  40.9 0.0 copy-done.3
  40.9 0.0 copy-done.5
  40.9 0.0 copy-done.6
  40.9 0.0 copy-done.4
  40.9 4.4 %collide.1 = f32[512,128]{1,0:T(8,128)S(1)} custom-call(f32[512,128]{1,0:T(8,128)S(1)} %bitcast.7, f32[24,8,640]{2,1,0:T(8,128)S(1)} %get-tuple-element.33.one_ref, f32[24,8,640]{2,1,0:T(8,128)S(1)} %get-tuple-element.34.two_ref, bf16[576,640]{1,0:T(8,128)(2,1)S(1)} %copy-done.3, bf16[640,576]{1,0:T(8,128)(2,1)S(1)} %copy-done, ...), custom_call_target="tpu_custom_call" | custom-call | tf_op jit(solution)/shard_map/collide/pallas_call | solution.py:559
  45.3 18.2 %all_to_all.23 = f32[32,16,128]{2,1,0:T(8,128)S(1)} all-to-all(f32[32,16,128]{2,1,0:T(8,128)S(1)} %bitcast.8), channel_id=1, replica_groups=mesh['space'=8,'vel'=32] {'vel'}, dimensions={0} | all-to-all | bytes 524288 | tf_op jit(solution)/shard_map/all_to_all | solution.py:635
  63.6 1.3 %add_collision.1 = f32[1,432,256]{2,1,0:T(8,128)} custom-call(bf16[128,256]{1,0:T(8,128)(2,1)S(1)} %get-tuple-element.21.pick_ref, f32[4,256,128]{2,1,0:T(8,128)S(1)} %get-tuple-element.31.cells_ref, f32[512,128]{1,0:T(8,128)S(1)} %bitcast.9), custom_call_target="tpu_custom_call" | custom-call | tf_op jit(solution)/shard_map/add_collision/pallas_call | solution.py:559
  (1 shorter events, 0.0 us)
Async XLA Ops:
  0.0 1.0 %copy-start.8 = (f32[1,256,432]{1,2,0:T(8,128)S(1)}, f32[1,256,432]{1,2,0:T(8,128)}, u32[]{:S(2)}) copy-start(f32[1,256,432]{1,2,0:T(8,128)} %param.15) | copy-start | bytes 1327108
  1.0 3.1 %copy-start.13 = (f32[13824]{0:T(1024)S(1)}, f32[13824]{0:T(1024)}, u32[]{:S(2)}) copy-start(f32[13824]{0:T(1024)} %param.21) | copy-start | bytes 165892
  1.3 6.1 %collective-permute-start.1 = (f32[560,128]{1,0:T(8,128)S(1)}, f32[560,128]{1,0:T(8,128)S(1)}, u32[]{:S(2)}, u32[]{:S(2)}) collective-permute-start(f32[560,128]{1,0:T(8,128)S(1)} %get-tuple-element.24.own_ref), channel_id=1, source_target_pairs={{0,224},{32,64},{64,32},{96,128},{128,96},{160,192},{192,160},{224... | collective-permute-start | bytes 860168 | tf_op jit(solution)/shard_map/ppermute | solution.py:574
  1.6 5.9 %collective-permute-start = (f32[560,128]{1,0:T(8,128)S(1)}, f32[560,128]{1,0:T(8,128)S(1)}, u32[]{:S(2)}, u32[]{:S(2)}) collective-permute-start(f32[560,128]{1,0:T(8,128)S(1)} %get-tuple-element.24.own_ref), channel_id=1, source_target_pairs={{0,32},{32,0},{64,96},{96,64},{128,160},{160,128},{192,224},{224,1... | collective-permute-start | bytes 860168 | tf_op jit(solution)/shard_map/ppermute | solution.py:574
  4.2 0.7 %copy-start.12 = (s32[256]{0:T(256)S(1)}, s32[256]{0:T(256)}, u32[]{:S(2)}) copy-start(s32[256]{0:T(256)} %param.18) | copy-start | bytes 3076
  4.8 7.4 %copy-start.10 = (f32[6,13824]{1,0:T(8,128)S(1)}, f32[6,13824]{1,0:T(8,128)}, u32[]{:S(2)}) copy-start(f32[6,13824]{1,0:T(8,128)} %second_ref.1) | copy-start | bytes 995332
  6.2 1.2 %copy-start.11 = (s32[1,4]{1,0:T(1,128)S(1)}, s32[1,4]{1,0:T(1,128)}, u32[]{:S(2)}) copy-start(s32[1,4]{1,0:T(1,128)} %near_ref.3) | copy-start | bytes 52
  6.2 6.0 %copy-start.1 = (bf16[640,640]{1,0:T(8,128)(2,1)S(1)}, bf16[640,640]{1,0:T(8,128)(2,1)}, u32[]{:S(2)}) copy-start(bf16[640,640]{1,0:T(8,128)(2,1)} %constant.19.clone.odd_ref) | copy-start | bytes 2457604
  6.2 6.0 %copy-start.2 = (bf16[640,640]{1,0:T(8,128)(2,1)S(1)}, bf16[640,640]{1,0:T(8,128)(2,1)}, u32[]{:S(2)}) copy-start(bf16[640,640]{1,0:T(8,128)(2,1)} %constant.18.clone.even_ref) | copy-start | bytes 2457604
  6.3 6.0 %copy-start.9 = (f32[6,13824]{1,0:T(8,128)S(1)}, f32[6,13824]{1,0:T(8,128)}, u32[]{:S(2)}) copy-start(f32[6,13824]{1,0:T(8,128)} %first_ref.1) | copy-start | bytes 995332
  8.9 6.1 %collective-permute-start.3 = (f32[560,128]{1,0:T(8,128)S(1)}, f32[560,128]{1,0:T(8,128)S(1)}, u32[]{:S(2)}, u32[]{:S(2)}) collective-permute-start(f32[560,128]{1,0:T(8,128)S(1)} %get-tuple-element.30.own_ref), channel_id=1, source_target_pairs={{0,224},{32,64},{64,32},{96,128},{128,96},{160,192},{192,160},{224... | collective-permute-start | bytes 860168 | tf_op jit(solution)/shard_map/ppermute | solution.py:574
  9.5 5.6 %collective-permute-start.2 = (f32[560,128]{1,0:T(8,128)S(1)}, f32[560,128]{1,0:T(8,128)S(1)}, u32[]{:S(2)}, u32[]{:S(2)}) collective-permute-start(f32[560,128]{1,0:T(8,128)S(1)} %get-tuple-element.30.own_ref), channel_id=1, source_target_pairs={{0,32},{32,0},{64,96},{96,64},{128,160},{160,128},{192,224},{224,1... | collective-permute-start | bytes 860168 | tf_op jit(solution)/shard_map/ppermute | solution.py:574
  13.6 27.2 %copy-start.7 = (bf16[4,256,256]{2,1,0:T(8,128)(2,1)S(1)}, bf16[4,256,256]{2,1,0:T(8,128)(2,1)}, u32[]{:S(2)}) copy-start(bf16[4,256,256]{2,1,0:T(8,128)(2,1)} %constant.20.clone.gh_ref) | copy-start | bytes 1572868
  15.1 25.8 %copy-start = (bf16[640,576]{1,0:T(8,128)(2,1)S(1)}, bf16[640,576]{1,0:T(8,128)(2,1)}, u32[]{:S(2)}) copy-start(bf16[640,576]{1,0:T(8,128)(2,1)} %constant.17.clone.unplace_ref) | copy-start | bytes 2211844
  15.1 25.8 %copy-start.3 = (bf16[576,640]{1,0:T(8,128)(2,1)S(1)}, bf16[576,640]{1,0:T(8,128)(2,1)}, u32[]{:S(2)}) copy-start(bf16[576,640]{1,0:T(8,128)(2,1)} %constant.16.clone.place_ref) | copy-start | bytes 2211844
  15.1 25.8 %copy-start.5 = (bf16[4,256,256]{2,1,0:T(8,128)(2,1)S(1)}, bf16[4,256,256]{2,1,0:T(8,128)(2,1)}, u32[]{:S(2)}) copy-start(bf16[4,256,256]{2,1,0:T(8,128)(2,1)} %constant.22.clone.ih_ref) | copy-start | bytes 1572868
  15.1 25.8 %copy-start.6 = (bf16[4,256,256]{2,1,0:T(8,128)(2,1)S(1)}, bf16[4,256,256]{2,1,0:T(8,128)(2,1)}, u32[]{:S(2)}) copy-start(bf16[4,256,256]{2,1,0:T(8,128)(2,1)} %constant.21.clone.gl_ref) | copy-start | bytes 1572868
  16.8 24.1 %copy-start.4 = (bf16[4,256,256]{2,1,0:T(8,128)(2,1)S(1)}, bf16[4,256,256]{2,1,0:T(8,128)(2,1)}, u32[]{:S(2)}) copy-start(bf16[4,256,256]{2,1,0:T(8,128)(2,1)} %constant.23.clone.il_ref) | copy-start | bytes 1572868

commit v3 on v2

--- a/solution.py
+++ b/solution.py
@@ -322,8 +322,9 @@
                 ]
 
 
-def last_kernel(pick_ref, cells_ref, got_ref, out_ref):
+def last_kernel(pick_ref, cells_ref, got_ref, out_ref, total_ref, done):
     pick = pick_ref[...]
+    copies = []
     for pair in range(2):
         got = jnp.concatenate(
             [
@@ -341,7 +342,16 @@
             tile = 2 * pair + side
             wide = TAIL if tile == TILES - 1 else LANES
             total = cells_ref[tile] + change[:, side * LANES : (side + 1) * LANES]
-            out_ref[0, tile * LANES : tile * LANES + wide, :] = total.T[:wide]
+            total_ref[tile] = total.T
+            copy = pltpu.make_async_copy(
+                total_ref.at[tile, pl.ds(0, wide), :],
+                out_ref.at[0, pl.ds(tile * LANES, wide), :],
+                done.at[tile],
+            )
+            copy.start()
+            copies.append(copy)
+    for copy in copies:
+        copy.wait()
 
 
 def order_kernel(first_ref, second_ref, loss_ref, even_ref, odd_ref, out_one, out_two, one_ref, two_ref):
@@ -633,7 +643,15 @@
         name="collide",
     )
     back = lax.all_to_all(collided, "vel", split_axis=0, concat_axis=0, tiled=True)
-    total = call(last_kernel, [], [pick, two, back], shape(1, WIDTH, CELLS), name="add_collision")
+    total = pl.pallas_call(
+        last_kernel,
+        out_shape=shape(1, WIDTH, CELLS),
+        in_specs=[BIG] * 3,
+        out_specs=pl.BlockSpec(memory_space=pl.ANY),
+        scratch_shapes=[pltpu.VMEM((TILES, LANES, CELLS), f32), pltpu.SemaphoreType.DMA((TILES,))],
+        compiler_params=PARAMS,
+        name="add_collision",
+    )(pick, two, back)
     return total.swapaxes(1, 2)
 
 

time: 65 us -> 65.1 us (level)
    pallas_call x8 -> x7, Pallas kernels: 13 us -> 11.8 us  [call(): pl.pallas_call(kernel, out_shape=outs, in_specs=[SMALL] * len(small) + [B...]
    pallas_call x0 -> x1, Pallas kernels: none -> 1.22 us  [shards(): pl.pallas_call(last_kernel, out_shape=shape(1, WIDTH, CELLS), in_specs=[B...]
where the time goes in v3:
time: 65.1 us; the launch traced here: 64.9 us
  blocking collectives  42.3 us (65%)
  Pallas kernels  13 us (20%)
  starting transfers between devices  5.5 us (8%)
  local copies, waits for them, and re-layouts  1.79 us (3%)
  waiting for transfers between devices  1.42 us (2%)
  between operations  0.97 us (1%)
    all_to_all x1, blocking collectives, shards(): got = lax.all_to_all(send, 'vel', split_axis=0, concat_axis=0, tiled=True)  24.1 us
    all_to_all x1, blocking collectives, shards(): lax.all_to_all(collided, 'vel', split_axis=0, concat_axis=0, tiled=True)  18.2 us
    pallas_call x7, Pallas kernels, call(): pl.pallas_call(kernel, out_shape=outs, in_specs=[SMALL] * len(small) + [B...  11.8 us
    ppermute x2, starting transfers between devices, swap_edges(): lax.ppermute(edge, 'space', pair)  4.71 us
    unnamed x28, local copies, waits for them, and re-layouts  1.75 us
    ppermute x2, waiting for transfers between devices, swap_edges(): lax.ppermute(edge, 'space', other)  1.41 us
  transfers between devices with their start and end apart: 4, of which 2 were waited for; matrix products, arithmetic and copies ran while one was open for 0% of the time, Pallas kernels for 6%

profile of v3, /device:TPU:24, one launch (start us, length us, event | category | flops | bytes accessed | tf_op | source)
XLA Modules:
  0.0 64.9 jit_solution(6369729153082281173)
XLA Ops:
  0.0 0.0 copy-start.8
  0.0 1.0 %copy-done.8 = f32[1,256,432]{1,2,0:T(8,128)S(1)} copy-done((f32[1,256,432]{1,2,0:T(8,128)S(1)}, f32[1,256,432]{1,2,0:T(8,128)}, u32[]{:S(2)}) %copy-start.8) | copy-done | bytes 442392
  1.0 0.0 copy-start.13
  1.0 0.3 pack_edges.1
  1.3 0.2 collective-permute-start.1
  1.6 1.9 %collective-permute-start = (f32[560,128]{1,0:T(8,128)S(1)}, f32[560,128]{1,0:T(8,128)S(1)}, u32[]{:S(2)}, u32[]{:S(2)}) collective-permute-start(f32[560,128]{1,0:T(8,128)S(1)} %get-tuple-element.24.own_ref), channel_id=1, source_target_pairs={{0,32},{32,0},{64,96},{96,64},{128,160},{160,128},{192,224},{224,1... | collective-permute-start | bytes 860168 | tf_op jit(solution)/shard_map/ppermute | solution.py:584
  4.1 0.0 copy-done.13
  4.2 0.0 copy-start.12
  4.2 0.7 %copy-done.12 = s32[256]{0:T(256)S(1)} copy-done((s32[256]{0:T(256)S(1)}, s32[256]{0:T(256)}, u32[]{:S(2)}) %copy-start.12) | copy-done | bytes 1048
  4.8 0.0 copy-start.10
  4.8 1.4 %first_inner.1 = (f32[2,4,16,16,128]{4,3,2,1,0:T(8,128)S(1)}, bf16[128,256]{1,0:T(8,128)(2,1)S(1)}) custom-call(s32[1,256]{1,0:T(1,128)S(1)} %bitcast.12, f32[4,256,128]{2,1,0:T(8,128)S(1)} %get-tuple-element.20.cells_ref.x_ref.base_ref), custom_call_target="tpu_custom_call" | custom-call | tf_op jit(solution)/shard_map/first_inner/pallas_call | solution.py:569
  6.2 0.0 copy-start.11
  6.2 0.0 copy-start.1
  6.2 0.0 copy-start.2
  6.3 0.0 copy-start.9
  6.3 1.2 %collective-permute-done.1.b_ref = f32[560,128]{1,0:T(8,128)S(1)} collective-permute-done((f32[560,128]{1,0:T(8,128)S(1)}, f32[560,128]{1,0:T(8,128)S(1)}, u32[]{:S(2)}, u32[]{:S(2)}) %collective-permute-start.1) | collective-permute-done | bytes 286752 | tf_op jit(solution)/shard_map/ppermute | solution.py:584
  7.4 0.0 collective-permute-done.a_ref
  7.4 0.0 copy-done.11
  7.4 1.5 %first_section.1 = (f32[4,256,128]{2,1,0:T(8,128)S(1)}, f32[560,128]{1,0:T(8,128)S(1)}) custom-call(s32[1,4]{1,0:T(1,128)S(1)} %copy-done.11, s32[1]{0:T(128)S(6)} %copy.16.level_ref, f32[4,256,128]{2,1,0:T(8,128)S(1)} %get-tuple-element.20.cells_ref.x_ref.base_ref, f32[2,4,16,16,128]{4,3,2,1,0:T(8,128)S(1)} %get-tuple-element.23.inner_ref, ...), custom_call_target="tpu_custom_call" | custom-call | tf_op jit(solution)/shard_map/first_section/pallas_call | solution.py:569
  8.9 0.6 collective-permute-start.3
  9.5 2.8 %collective-permute-start.2 = (f32[560,128]{1,0:T(8,128)S(1)}, f32[560,128]{1,0:T(8,128)S(1)}, u32[]{:S(2)}, u32[]{:S(2)}) collective-permute-start(f32[560,128]{1,0:T(8,128)S(1)} %get-tuple-element.30.own_ref), channel_id=1, source_target_pairs={{0,32},{32,0},{64,96},{96,64},{128,160},{160,128},{192,224},{224,1... | collective-permute-start | bytes 860168 | tf_op jit(solution)/shard_map/ppermute | solution.py:584
  12.3 0.0 copy-done.10
  12.3 0.0 copy-done.1
  12.3 0.0 copy-done.2
  12.3 0.0 copy-done.9
  12.3 1.3 %order_weights.1 = (f32[24,8,640]{2,1,0:T(8,128)S(1)}, f32[24,8,640]{2,1,0:T(8,128)S(1)}) custom-call(f32[6,13824]{1,0:T(8,128)S(1)} %copy-done.9, f32[6,13824]{1,0:T(8,128)S(1)} %copy-done.10, f32[1,13824]{1,0:T(1,128)S(1)} %reshape.11.loss_ref, bf16[640,640]{1,0:T(8,128)(2,1)S(1)} %copy-done.2, bf16[640,640]{1,0:T(8,128)(2,1)S(1)} %copy-done.1), custom_call_target="tpu_custom_call" | custom-call | tf_op jit(solution)/shard_map/order_weights/pallas_call | solution.py:569
  13.6 0.0 copy-start.7
  13.7 1.2 %second_inner.1.inner_ref = f32[2,4,16,16,128]{4,3,2,1,0:T(8,128)S(1)} custom-call(f32[4,256,128]{2,1,0:T(8,128)S(1)} %get-tuple-element.25.cells_ref.x_ref), custom_call_target="tpu_custom_call" | custom-call | tf_op jit(solution)/shard_map/second_inner/pallas_call | solution.py:569
  14.8 0.2 collective-permute-done.3.b_ref
  15.1 0.0 collective-permute-done.2.a_ref
  15.1 0.0 copy-start
  15.1 0.0 copy-start.3
  15.1 0.0 copy-start.5
  15.1 0.0 copy-start.6
  15.1 1.7 %second_section.1 = (f32[4,256,128]{2,1,0:T(8,128)S(1)}, f32[512,128]{1,0:T(8,128)S(1)}) custom-call(s32[1,4]{1,0:T(1,128)S(1)} %copy-done.11, s32[1]{0:T(128)S(6)} %copy.16.level_ref, bf16[128,256]{1,0:T(8,128)(2,1)S(1)} %get-tuple-element.21.pick_ref, f32[4,256,128]{2,1,0:T(8,128)S(1)} %get-tuple-element.20.cells_ref.x_ref.base_ref, ...), custom_call_target="tpu_custom_call" | custom-call | tf_op jit(solution)/shard_map/second_section/pallas_call | solution.py:569
  16.8 0.0 copy-start.4
  16.8 24.1 %all_to_all.22 = f32[32,16,128]{2,1,0:T(8,128)S(1)} all-to-all(f32[32,16,128]{2,1,0:T(8,128)S(1)} %bitcast.11), channel_id=1, replica_groups=mesh['space'=8,'vel'=32] {'vel'}, dimensions={0} | all-to-all | bytes 524288 | tf_op jit(solution)/shard_map/all_to_all | solution.py:629
  40.9 0.0 copy-done.7
  40.9 0.0 copy-done
  40.9 0.0 copy-done.3
  40.9 0.0 copy-done.5
  40.9 0.0 copy-done.6
  40.9 0.0 copy-done.4
  40.9 4.4 %collide.1 = f32[512,128]{1,0:T(8,128)S(1)} custom-call(f32[512,128]{1,0:T(8,128)S(1)} %bitcast.7, f32[24,8,640]{2,1,0:T(8,128)S(1)} %get-tuple-element.33.one_ref, f32[24,8,640]{2,1,0:T(8,128)S(1)} %get-tuple-element.34.two_ref, bf16[576,640]{1,0:T(8,128)(2,1)S(1)} %copy-done.3, bf16[640,576]{1,0:T(8,128)(2,1)S(1)} %copy-done, ...), custom_call_target="tpu_custom_call" | custom-call | tf_op jit(solution)/shard_map/collide/pallas_call | solution.py:569
  45.3 18.2 %all_to_all.23 = f32[32,16,128]{2,1,0:T(8,128)S(1)} all-to-all(f32[32,16,128]{2,1,0:T(8,128)S(1)} %bitcast.8), channel_id=1, replica_groups=mesh['space'=8,'vel'=32] {'vel'}, dimensions={0} | all-to-all | bytes 524288 | tf_op jit(solution)/shard_map/all_to_all | solution.py:645
  63.5 1.2 %add_collision.1 = f32[1,432,256]{2,1,0:T(8,128)} custom-call(bf16[128,256]{1,0:T(8,128)(2,1)S(1)} %get-tuple-element.21.pick_ref, f32[4,256,128]{2,1,0:T(8,128)S(1)} %get-tuple-element.31.cells_ref, f32[512,128]{1,0:T(8,128)S(1)} %bitcast.9), custom_call_target="tpu_custom_call" | custom-call | tf_op jit(solution)/shard_map/add_collision/pallas_call | solution.py:646
  (1 shorter events, 0.0 us)
Async XLA Ops:
  0.0 1.0 %copy-start.8 = (f32[1,256,432]{1,2,0:T(8,128)S(1)}, f32[1,256,432]{1,2,0:T(8,128)}, u32[]{:S(2)}) copy-start(f32[1,256,432]{1,2,0:T(8,128)} %param.15) | copy-start | bytes 1327108
  1.0 3.1 %copy-start.13 = (f32[13824]{0:T(1024)S(1)}, f32[13824]{0:T(1024)}, u32[]{:S(2)}) copy-start(f32[13824]{0:T(1024)} %param.21) | copy-start | bytes 165892
  1.3 6.1 %collective-permute-start.1 = (f32[560,128]{1,0:T(8,128)S(1)}, f32[560,128]{1,0:T(8,128)S(1)}, u32[]{:S(2)}, u32[]{:S(2)}) collective-permute-start(f32[560,128]{1,0:T(8,128)S(1)} %get-tuple-element.24.own_ref), channel_id=1, source_target_pairs={{0,224},{32,64},{64,32},{96,128},{128,96},{160,192},{192,160},{224... | collective-permute-start | bytes 860168 | tf_op jit(solution)/shard_map/ppermute | solution.py:584
  1.6 5.9 %collective-permute-start = (f32[560,128]{1,0:T(8,128)S(1)}, f32[560,128]{1,0:T(8,128)S(1)}, u32[]{:S(2)}, u32[]{:S(2)}) collective-permute-start(f32[560,128]{1,0:T(8,128)S(1)} %get-tuple-element.24.own_ref), channel_id=1, source_target_pairs={{0,32},{32,0},{64,96},{96,64},{128,160},{160,128},{192,224},{224,1... | collective-permute-start | bytes 860168 | tf_op jit(solution)/shard_map/ppermute | solution.py:584
  4.2 0.7 %copy-start.12 = (s32[256]{0:T(256)S(1)}, s32[256]{0:T(256)}, u32[]{:S(2)}) copy-start(s32[256]{0:T(256)} %param.18) | copy-start | bytes 3076
  4.8 7.4 %copy-start.10 = (f32[6,13824]{1,0:T(8,128)S(1)}, f32[6,13824]{1,0:T(8,128)}, u32[]{:S(2)}) copy-start(f32[6,13824]{1,0:T(8,128)} %second_ref.1) | copy-start | bytes 995332
  6.2 1.2 %copy-start.11 = (s32[1,4]{1,0:T(1,128)S(1)}, s32[1,4]{1,0:T(1,128)}, u32[]{:S(2)}) copy-start(s32[1,4]{1,0:T(1,128)} %near_ref.3) | copy-start | bytes 52
  6.2 6.0 %copy-start.1 = (bf16[640,640]{1,0:T(8,128)(2,1)S(1)}, bf16[640,640]{1,0:T(8,128)(2,1)}, u32[]{:S(2)}) copy-start(bf16[640,640]{1,0:T(8,128)(2,1)} %constant.19.clone.odd_ref) | copy-start | bytes 2457604
  6.2 6.0 %copy-start.2 = (bf16[640,640]{1,0:T(8,128)(2,1)S(1)}, bf16[640,640]{1,0:T(8,128)(2,1)}, u32[]{:S(2)}) copy-start(bf16[640,640]{1,0:T(8,128)(2,1)} %constant.18.clone.even_ref) | copy-start | bytes 2457604
  6.3 6.0 %copy-start.9 = (f32[6,13824]{1,0:T(8,128)S(1)}, f32[6,13824]{1,0:T(8,128)}, u32[]{:S(2)}) copy-start(f32[6,13824]{1,0:T(8,128)} %first_ref.1) | copy-start | bytes 995332
  8.9 6.1 %collective-permute-start.3 = (f32[560,128]{1,0:T(8,128)S(1)}, f32[560,128]{1,0:T(8,128)S(1)}, u32[]{:S(2)}, u32[]{:S(2)}) collective-permute-start(f32[560,128]{1,0:T(8,128)S(1)} %get-tuple-element.30.own_ref), channel_id=1, source_target_pairs={{0,224},{32,64},{64,32},{96,128},{128,96},{160,192},{192,160},{224... | collective-permute-start | bytes 860168 | tf_op jit(solution)/shard_map/ppermute | solution.py:584
  9.5 5.6 %collective-permute-start.2 = (f32[560,128]{1,0:T(8,128)S(1)}, f32[560,128]{1,0:T(8,128)S(1)}, u32[]{:S(2)}, u32[]{:S(2)}) collective-permute-start(f32[560,128]{1,0:T(8,128)S(1)} %get-tuple-element.30.own_ref), channel_id=1, source_target_pairs={{0,32},{32,0},{64,96},{96,64},{128,160},{160,128},{192,224},{224,1... | collective-permute-start | bytes 860168 | tf_op jit(solution)/shard_map/ppermute | solution.py:584
  13.6 27.2 %copy-start.7 = (bf16[4,256,256]{2,1,0:T(8,128)(2,1)S(1)}, bf16[4,256,256]{2,1,0:T(8,128)(2,1)}, u32[]{:S(2)}) copy-start(bf16[4,256,256]{2,1,0:T(8,128)(2,1)} %constant.20.clone.gh_ref) | copy-start | bytes 1572868
  15.1 25.8 %copy-start = (bf16[640,576]{1,0:T(8,128)(2,1)S(1)}, bf16[640,576]{1,0:T(8,128)(2,1)}, u32[]{:S(2)}) copy-start(bf16[640,576]{1,0:T(8,128)(2,1)} %constant.17.clone.unplace_ref) | copy-start | bytes 2211844
  15.1 25.8 %copy-start.3 = (bf16[576,640]{1,0:T(8,128)(2,1)S(1)}, bf16[576,640]{1,0:T(8,128)(2,1)}, u32[]{:S(2)}) copy-start(bf16[576,640]{1,0:T(8,128)(2,1)} %constant.16.clone.place_ref) | copy-start | bytes 2211844
  15.1 25.8 %copy-start.5 = (bf16[4,256,256]{2,1,0:T(8,128)(2,1)S(1)}, bf16[4,256,256]{2,1,0:T(8,128)(2,1)}, u32[]{:S(2)}) copy-start(bf16[4,256,256]{2,1,0:T(8,128)(2,1)} %constant.22.clone.ih_ref) | copy-start | bytes 1572868
  15.1 25.8 %copy-start.6 = (bf16[4,256,256]{2,1,0:T(8,128)(2,1)S(1)}, bf16[4,256,256]{2,1,0:T(8,128)(2,1)}, u32[]{:S(2)}) copy-start(bf16[4,256,256]{2,1,0:T(8,128)(2,1)} %constant.21.clone.gl_ref) | copy-start | bytes 1572868
  16.8 24.1 %copy-start.4 = (bf16[4,256,256]{2,1,0:T(8,128)(2,1)S(1)}, bf16[4,256,256]{2,1,0:T(8,128)(2,1)}, u32[]{:S(2)}) copy-start(bf16[4,256,256]{2,1,0:T(8,128)(2,1)} %constant.23.clone.il_ref) | copy-start | bytes 1572868
